TPU v7x, 128 devices: a whole 4x4x4 slice. The times are simulated.
128 devices in a mesh: tile: 32 (over y, z_hi, x), band: 4 (over z_lo, core).
Axes of the slice: x: 4, y: 4, z: 4 (z_hi: 2, z_lo: 2; z = z_hi * 2 + z_lo), core: 2. Of those that a mesh axis runs over, the one named last changes fastest.
Arguments:
- source_cells: bfloat16 [131072, 256], P(('tile', 'band')), may hold values from -6 to 6
- regrid_weights: bfloat16 [16384, 16, 64], P(('tile', 'band')), may hold values from -0.5 to 0.5
- pair_target: int32 [16384, 1], P(('tile', 'band')), may hold values from 0 to 127; in each aligned block of 128 rows (0 to 127, 128 to 255, ...) at most 2 rows name the same one
- pair_block: int32 [16384], P(('tile', 'band')), may hold values from 0 to 63
- pair_source: int32 [16384], P(('tile', 'band')), may hold values from 0 to 15
- flip_codes: int32 [32], replicated, may hold values from 0 to 1
- kernel_one: bfloat16 [3, 3, 256, 256], replicated, may hold values from -0.125 to 0.125
- kernel_two: bfloat16 [3, 3, 256, 256], replicated, may hold values from -0.125 to 0.125
- out_grad: bfloat16 [32, 32, 128, 256], P('tile', 'band'), may hold values from -6 to 6
Outputs:
- mixed_out: bfloat16 [32, 32, 128, 256], P('tile', 'band')
- kernel_one_grad: float32 [3, 3, 256, 256], replicated
- kernel_two_grad: float32 [3, 3, 256, 256], replicated
- source_grad: bfloat16 [131072, 256], P(('tile', 'band'))
Inputs may be any that keep to these rules, and one draw needn't show every extreme that they name: `pair_target`: within the 128 pairs of one device no target device is named more than 2 times, and some target device exactly 2 times.
All inputs are finite; a program needn't handle non-finite values.
Results may differ from a plain program's by a relative error of at most 0.0065.
Values may be sent and summed in bfloat16 or wider, within the bound.
A program may use at most 128 MiB of HBM per device.

v0:
```python
import jax
import jax.numpy as jnp
from jax import lax
from jax.experimental import pallas as pl
from jax.experimental.pallas import tpu as pltpu
from jax.sharding import PartitionSpec as P

F32 = jnp.float32
BF16 = jnp.bfloat16
MESH = pl.DeviceIdType.MESH
VM = pl.BlockSpec(memory_space=pltpu.VMEM)
SM = pl.BlockSpec(memory_space=pltpu.SMEM)
LIMIT = 48 * 2**20
ROWS, COLS, CH = 8, 128, 256
PAIRS, BT, BL, SB, BLOCKS = 128, 16, 64, 16, 64
CELLS = ROWS * COLS


def params(**more):
    return pltpu.CompilerParams(vmem_limit_bytes=LIMIT, **more)


def regrid_kernel(tgt, psrc, w_ref, src_ref, out_ref, slot_ref, cnt, masks, wexp):
    lane = lax.broadcasted_iota(jnp.int32, (BT, 128), 1)
    masks[0] = (lane < BL).astype(F32).astype(BF16)
    masks[1] = (lane >= BL).astype(F32).astype(BF16)
    wexp[...] = jnp.zeros_like(wexp)

    def clear(i, c):
        cnt[i] = 0
        return c

    lax.fori_loop(0, PAIRS, clear, 0)

    def rank(p, c):
        t = tgt[p]
        r = cnt[t]
        cnt[t] = r + 1
        slot_ref[p] = jnp.minimum(2 * t + r, 2 * PAIRS - 1)
        return c

    lax.fori_loop(0, PAIRS, rank, 0)

    def place(p, c):
        s = psrc[p]
        w = w_ref[p]
        ww = jnp.concatenate([w, w], axis=1) * masks[lax.rem(s, 2)]
        row = pl.multiple_of(p * BT, BT)
        col = pl.multiple_of((s // 2) * 128, 128)
        wexp[pl.ds(row, BT), pl.ds(col, 128)] = ww
        return c

    lax.fori_loop(0, PAIRS, place, 0, unroll=4)
    out_ref[...] = jnp.zeros_like(out_ref)
    for m in range(4):
        part = jnp.dot(wexp[m * 512 : (m + 1) * 512, :], src_ref[...], preferred_element_type=F32).astype(BF16)
        for q in range(32):
            out_ref[slot_ref[m * 32 + q]] = part[q * BT : (q + 1) * BT]


def regrid(tgt, psrc, weights, source):
    return pl.pallas_call(
        regrid_kernel,
        name="regrid",
        out_shape=(
            jax.ShapeDtypeStruct((2 * PAIRS, BT, CH), BF16),
            jax.ShapeDtypeStruct((PAIRS,), jnp.int32),
        ),
        in_specs=[SM, SM, VM, VM],
        out_specs=(VM, SM),
        scratch_shapes=[
            pltpu.SMEM((PAIRS,), jnp.int32),
            pltpu.VMEM((2, BT, 128), BF16),
            pltpu.VMEM((PAIRS * BT, SB * BL), BF16),
        ],
        compiler_params=params(),
        cost_estimate=pl.CostEstimate(flops=2 * 2048 * 1024 * 256, bytes_accessed=6 * 2**20, transcendentals=0),
    )(tgt, psrc, weights, source)


def gather_sum_kernel(ids, got_ref, out_ref, acc):
    acc[...] = jnp.zeros_like(acc)

    def add(q, c):
        k = ids[q]
        acc[k] += got_ref[q].astype(F32)
        return c

    lax.fori_loop(0, 2 * PAIRS, add, 0, unroll=8)
    out_ref[...] = acc[0:BLOCKS].astype(BF16)


def gather_sum(ids, arrived):
    return pl.pallas_call(
        gather_sum_kernel,
        name="gather_sum",
        out_shape=jax.ShapeDtypeStruct((BLOCKS, BT, CH), BF16),
        in_specs=[SM, VM],
        out_specs=VM,
        scratch_shapes=[pltpu.VMEM((BLOCKS + 1, BT, CH), F32)],
        compiler_params=params(),
        cost_estimate=pl.CostEstimate(flops=2**21, bytes_accessed=3 * 2**20, transcendentals=0),
    )(ids, arrived)


def place_in_mesh():
    return lax.axis_index("tile"), lax.axis_index("band"), lax.axis_size("tile"), lax.axis_size("band")


def greet(others=0):
    t, b, tiles, bands = place_in_mesh()
    barrier = pltpu.get_barrier_semaphore()
    for dt in (1, -1, 0):
        for db in (-1, 0, 1):
            if dt == 0 and db == 0:
                continue

            def say(dt=dt, db=db):
                pl.semaphore_signal(
                    barrier, inc=1, device_id=(lax.rem(t + dt + tiles, tiles), b + db), device_id_type=MESH
                )

            near_band(b, bands, db, say)
    near = 2 + jnp.where(b > 0, 3, 0) + jnp.where(b < bands - 1, 3, 0)
    pl.semaphore_wait(barrier, near + others)


def near_band(b, bands, db, action):
    if db == 0:
        action()
    elif db < 0:
        pl.when(b > 0)(action)
    else:
        pl.when(b < bands - 1)(action)


def side_copy(send, recv, ss, rs, way, db, group):
    t, b, tiles, bands = place_in_mesh()
    to = lax.rem(t + (1 if way == 0 else tiles - 1), tiles)
    return pltpu.make_async_remote_copy(
        src_ref=send.at[way],
        dst_ref=recv.at[way, group],
        send_sem=ss.at[way, 1 + db],
        recv_sem=rs.at[way, group],
        device_id=(to, b + db),
        device_id_type=MESH,
    )


def row_copy(ext, d, ss, rs, db):
    t, b, tiles, bands = place_in_mesh()
    if db < 0:
        src, dst, k = ext.at[pl.ds(d, d)], ext.at[pl.ds(ROWS + d, d)], 0
    else:
        src, dst, k = ext.at[pl.ds(ROWS, d)], ext.at[pl.ds(0, d)], 1
    return pltpu.make_async_remote_copy(
        src_ref=src, dst_ref=dst, send_sem=ss.at[k], recv_sem=rs.at[k], device_id=(t, b + db), device_id_type=MESH
    )


def start_sides(send, recv, ss, rs):
    b, bands = lax.axis_index("band"), lax.axis_size("band")
    for way in (0, 1):
        for db in (0, -1, 1):
            near_band(b, bands, db, lambda way=way, db=db: side_copy(send, recv, ss, rs, way, db, 1 - db).start())


def start_rows(ext, d, ss, rs):
    b, bands = lax.axis_index("band"), lax.axis_size("band")
    for db in (-1, 1):
        near_band(b, bands, db, lambda db=db: row_copy(ext, d, ss, rs, db).start())


def wait_sides_recv(send, recv, ss, rs):
    b, bands = lax.axis_index("band"), lax.axis_size("band")
    for way in (0, 1):
        for db in (0, -1, 1):
            near_band(b, bands, db, lambda way=way, db=db: side_copy(send, recv, ss, rs, way, 0, 1 + db).wait_recv())


def wait_sides_send(send, recv, ss, rs):
    b, bands = lax.axis_index("band"), lax.axis_size("band")
    for way in (0, 1):
        for db in (0, -1, 1):
            near_band(b, bands, db, lambda way=way, db=db: side_copy(send, recv, ss, rs, way, db, 1 - db).wait_send())


def wait_rows_recv(ext, d, ss, rs):
    b, bands = lax.axis_index("band"), lax.axis_size("band")
    near_band(b, bands, -1, lambda: row_copy(ext, d, ss, rs, 1).wait_recv())
    near_band(b, bands, 1, lambda: row_copy(ext, d, ss, rs, -1).wait_recv())


def wait_rows_send(ext, d, ss, rs):
    b, bands = lax.axis_index("band"), lax.axis_size("band")
    for db in (-1, 1):
        near_band(b, bands, db, lambda db=db: row_copy(ext, d, ss, rs, db).wait_send())


def clear_edges(ext, d):
    b, bands = lax.axis_index("band"), lax.axis_size("band")

    @pl.when(b == 0)
    def _():
        ext[0:d] = jnp.zeros((d, COLS, CH), BF16)

    @pl.when(b == bands - 1)
    def _():
        ext[ROWS + d : ROWS + 2 * d] = jnp.zeros((d, COLS, CH), BF16)


def clear_groups(recv):
    b, bands = lax.axis_index("band"), lax.axis_size("band")
    for way in (0, 1):

        @pl.when(b == 0)
        def _():
            recv[way, 0] = jnp.zeros(recv.shape[2:], BF16)

        @pl.when(b == bands - 1)
        def _():
            recv[way, 2] = jnp.zeros(recv.shape[2:], BF16)


def flags(flip):
    t, b, tiles, bands = place_in_mesh()
    me = flip[t]
    before = flip[lax.rem(t + tiles - 1, tiles)]
    after = flip[lax.rem(t + 1, tiles)]
    return me, before, after


def make_slab(ext, d, send, base, flip_me, tmp):
    if d == 1:
        tmp[...] = jnp.zeros_like(tmp)
    for r in range(ROWS):
        first = ext[d + r, 0:16, :].astype(F32)
        last = ext[d + r, COLS - 16 : COLS, :].astype(F32)
        for k in range(d):
            tmp[0, k * 8 + r : k * 8 + r + 1, :] = first[k : k + 1]
            tmp[1, k * 8 + r : k * 8 + r + 1, :] = last[15 - k : 16 - k]
    turned = jnp.full((16, CH), flip_me, jnp.int32) == 1
    left, right = tmp[0], tmp[1]
    send[0, base : base + 16] = jnp.where(turned, left, right).astype(BF16)
    send[1, base : base + 16] = jnp.where(turned, right, left).astype(BF16)


def open_slab(recv, d, base, flip_me, rim):
    turned = jnp.full((16, CH), flip_me, jnp.int32) == 1
    for g in range(3):
        before = recv[0, g, base : base + 16].astype(F32)
        after = recv[1, g, base : base + 16].astype(F32)
        sides = (jnp.where(turned, after, before), jnp.where(turned, before, after))
        for side in (0, 1):
            for k in range(d):
                part = sides[side][k * 8 : k * 8 + 8]
                if g == 0:
                    rim[side, k, 0:d, :] = part[8 - d :]
                elif g == 1:
                    rim[side, k, d : d + 8, :] = part
                else:
                    rim[side, k, d + 8 : 2 * d + 8, :] = part[:d]


def split_rim(rim, d, flip_me, flip_before, flip_after, turned_rim):
    odd_before = (flip_before != flip_me).astype(jnp.int32)
    odd_after = (flip_after != flip_me).astype(jnp.int32)
    odd_left = jnp.where(flip_me == 0, odd_before, odd_after)
    odd_right = jnp.where(flip_me == 0, odd_after, odd_before)
    for side, odd in ((0, odd_left), (1, odd_right)):
        mask = jnp.full((16, CH), odd, jnp.int32) == 1
        for k in range(d):
            whole = rim[side, k]
            turned_rim[side, k] = jnp.where(mask, whole, 0.0)
            rim[side, k] = jnp.where(mask, 0.0, whole)


def widen(ext, d, rim, wide):
    col = lax.broadcasted_iota(jnp.int32, (COLS, CH), 0)

    def one(row, carry):
        mid = ext[row]
        x = mid.astype(F32)
        left = pltpu.roll(x, d, 0)
        right = pltpu.roll(x, COLS - d, 0)
        for k in range(d):
            near = jnp.broadcast_to(rim[0, k, pl.ds(row, 1), :], (COLS, CH))
            left = jnp.where(col == d - 1 - k, near, left)
            near = jnp.broadcast_to(rim[1, k, pl.ds(row, 1), :], (COLS, CH))
            right = jnp.where(col == COLS - d + k, near, right)
        at = pl.ds(pl.multiple_of(row * COLS, COLS), COLS)
        wide[at, 0:CH] = left.astype(BF16)
        wide[at, CH : 2 * CH] = mid
        wide[at, 2 * CH : 3 * CH] = right.astype(BF16)
        return carry

    lax.fori_loop(0, ROWS + 2 * d, one, 0)


def conv_block(wide, d, taps, m, rows):
    total = None
    for i in range(3):
        lhs = wide[pl.ds(pl.multiple_of(m + i * d * COLS, COLS), rows), :]
        part = jnp.dot(lhs, taps[i], preferred_element_type=F32)
        total = part if total is None else total + part
    return total


def turned_part(turned_rim, d, taps, out):
    left, right = None, None
    for i in range(3):
        lhs_left = jnp.concatenate([turned_rim[0, d - 1 - c, i * d : i * d + 8, :] for c in range(d)], axis=0)
        lhs_right = jnp.concatenate([turned_rim[1, c, i * d : i * d + 8, :] for c in range(d)], axis=0)
        a = jnp.dot(lhs_left.astype(BF16), taps[i, 2 * CH : 3 * CH, :], preferred_element_type=F32)
        z = jnp.dot(lhs_right.astype(BF16), taps[i, 0:CH, :], preferred_element_type=F32)
        left = a if left is None else left + a
        right = z if right is None else right + z
    for c in range(d):
        for r in range(ROWS):
            at = r * COLS + c
            out[at : at + 1, :] += left[c * 8 + r : c * 8 + r + 1]
            at = r * COLS + COLS - d + c
            out[at : at + 1, :] += right[c * 8 + r : c * 8 + r + 1]


STEP = 256


def spot(t, b):
    x = lax.rem(t, 4)
    y = lax.div(t, 8)
    z = lax.rem(lax.div(t, 4), 2) * 2 + lax.div(b, 2)
    return x, y, z, lax.rem(b, 2)


def device_at(x, y, z, core):
    return (y * 8 + lax.div(z, 2) * 4 + x, lax.rem(z, 2) * 2 + core)


def table_peer(stage, k):
    t, b, tiles, bands = place_in_mesh()
    x, y, z, core = spot(t, b)
    if stage == 0:
        return (t, lax.rem(b + k, 4))
    if stage == 1:
        return (t - x + lax.rem(x + k, 4), b)
    if stage == 2:
        return (t + 4 - 8 * lax.rem(lax.div(t, 4), 2), b)
    return (lax.rem(t + 8 * k, 32), b)


TABLE_PEERS = (3, 3, 1, 3)
TABLE_ROWS = (1, 4, 16, 32)


def table_copy(tab, ss, rs, stage, k):
    t, b, tiles, bands = place_in_mesh()
    n = TABLE_ROWS[stage]
    at = lax.div(t * 4 + b, n) * n
    rows = tab.at[pl.ds(at, n)]
    return pltpu.make_async_remote_copy(
        src_ref=rows, dst_ref=rows, send_sem=ss.at[stage, k - 1], recv_sem=rs.at[stage, k - 1],
        device_id=table_peer(stage, k), device_id_type=MESH,
    )


def table_start(tab, ss, rs, stage):
    for k in range(1, TABLE_PEERS[stage] + 1):
        table_copy(tab, ss, rs, stage, k).start()


def table_wait(tab, ss, rs, stage):
    for k in range(1, TABLE_PEERS[stage] + 1):
        table_copy(tab, ss, rs, stage, k).wait()


def greet_table():
    barrier = pltpu.get_barrier_semaphore()
    for stage in range(4):
        for k in range(1, TABLE_PEERS[stage] + 1):
            pl.semaphore_signal(barrier, inc=1, device_id=table_peer(stage, k), device_id_type=MESH)


def back_kernel(
    flip, own_ref, g_ref, k1_ref, k2_ref, hg_ref, k1t_ref, tab,
    ext, send, recv, tmp, rim, trim, wide, k2t, ss, rs, rss, rrs, tss, trs,
):
    d = 2
    t, b, tiles, bands = place_in_mesh()
    tab[t * 4 + b] = own_ref[...]
    me, before, after = flags(flip)
    ext[pl.ds(d, ROWS)] = g_ref[...]
    make_slab(ext, d, send, 0, me, tmp)
    clear_edges(ext, d)
    clear_groups(recv)
    greet_table()
    greet(sum(TABLE_PEERS))
    table_start(tab, tss, trs, 0)
    start_sides(send, recv, ss, rs)
    start_rows(ext, d, rss, rrs)
    for i in range(3):
        for j in range(3):
            k2t[i, j * CH : (j + 1) * CH, :] = k2_ref[2 - i, 2 - j].T
            k1t_ref[i, j * CH : (j + 1) * CH, :] = k1_ref[2 - i, 2 - j].T
    table_wait(tab, tss, trs, 0)
    table_start(tab, tss, trs, 1)
    wait_sides_recv(send, recv, ss, rs)
    wait_rows_recv(ext, d, rss, rrs)
    open_slab(recv, d, 0, me, rim)
    split_rim(rim, d, me, before, after, trim)
    widen(ext, d, rim, wide)
    table_wait(tab, tss, trs, 1)
    table_start(tab, tss, trs, 2)

    def block(n, carry):
        m = pl.multiple_of(n * STEP, STEP)
        hg_ref[pl.ds(m, STEP), :] = conv_block(wide, d, k2t, m, STEP)
        return carry

    lax.fori_loop(0, CELLS // STEP, block, 0)
    table_wait(tab, tss, trs, 2)
    table_start(tab, tss, trs, 3)
    turned_part(trim, d, k2t, hg_ref)
    table_wait(tab, tss, trs, 3)
    wait_sides_send(send, recv, ss, rs)
    wait_rows_send(ext, d, rss, rrs)


def back(flip, own, grad, k1, k2):
    d = 2
    return pl.pallas_call(
        back_kernel,
        name="hidden_adjoint",
        out_shape=(
            jax.ShapeDtypeStruct((CELLS, CH), F32),
            jax.ShapeDtypeStruct((3, 3 * CH, CH), BF16),
            jax.ShapeDtypeStruct((PAIRS, 1, PAIRS), jnp.int32),
        ),
        in_specs=[SM, VM, VM, VM, VM],
        out_specs=(VM, VM, VM),
        scratch_shapes=[
            pltpu.VMEM((ROWS + 2 * d, COLS, CH), BF16),
            pltpu.VMEM((2, 16, CH), BF16),
            pltpu.VMEM((2, 3, 16, CH), BF16),
            pltpu.VMEM((2, 16, CH), F32),
            pltpu.VMEM((2, d, 16, CH), F32),
            pltpu.VMEM((2, d, 16, CH), F32),
            pltpu.VMEM(((ROWS + 2 * d) * COLS, 3 * CH), BF16),
            pltpu.VMEM((3, 3 * CH, CH), BF16),
            pltpu.SemaphoreType.DMA((2, 3)),
            pltpu.SemaphoreType.DMA((2, 3)),
            pltpu.SemaphoreType.DMA((2,)),
            pltpu.SemaphoreType.DMA((2,)),
            pltpu.SemaphoreType.DMA((4, 3)),
            pltpu.SemaphoreType.DMA((4, 3)),
        ],
        compiler_params=params(collective_id=1, has_side_effects=True),
        cost_estimate=pl.CostEstimate(flops=6 * 2**30, bytes_accessed=8 * 2**20, transcendentals=0),
    )(flip, own, grad, k1, k2)


def mid_kernel(
    flip, ids, x_ref, hg_ref, g_ref, k1_ref, k1t_ref,
    back_ref, wide1_ref, wide2_ref, pg_ref,
    ext, exth, extp, send, recv, send2, recv2, tmp, rim, rim2, trim, widep, ing, rounded,
    ss, rs, rss, rrs, ss2, rs2, rssh, rrsh, rssp, rrsp,
):
    me, before, after = flags(flip)
    ext[pl.ds(1, ROWS)] = x_ref[...]
    make_slab(ext, 1, send, 0, me, tmp)
    clear_edges(ext, 1)
    clear_edges(exth, 2)
    clear_edges(extp, 1)
    clear_groups(recv)
    clear_groups(recv2)
    greet()
    start_sides(send, recv, ss, rs)
    start_rows(ext, 1, rss, rrs)
    wait_sides_recv(send, recv, ss, rs)
    wait_rows_recv(ext, 1, rss, rrs)
    open_slab(recv, 1, 0, me, rim)
    widen(ext, 1, rim, wide1_ref)

    def act(n, carry):
        m = pl.multiple_of(n * STEP, STEP)
        pre = conv_block(wide1_ref, 1, k1_ref, m, STEP)
        s = jax.nn.sigmoid(pre)
        hid = (pre * s).astype(BF16)
        grad = (hg_ref[pl.ds(m, STEP), :] * s * (1.0 + pre * (1.0 - s))).astype(BF16)
        for q in range(STEP // COLS):
            row = n * (STEP // COLS) + q
            exth[2 + row] = hid[q * COLS : (q + 1) * COLS]
            extp[1 + row] = grad[q * COLS : (q + 1) * COLS]
        pg_ref[pl.ds(m, STEP), :] = grad
        return carry

    lax.fori_loop(0, CELLS // STEP, act, 0)
    make_slab(extp, 1, send2, 16, me, tmp)
    make_slab(exth, 2, send2, 0, me, tmp)
    start_sides(send2, recv2, ss2, rs2)
    start_rows(extp, 1, rssp, rrsp)
    start_rows(exth, 2, rssh, rrsh)
    wait_sides_recv(send2, recv2, ss2, rs2)
    wait_rows_recv(extp, 1, rssp, rrsp)
    open_slab(recv2, 1, 16, me, rim)
    split_rim(rim, 1, me, before, after, trim)
    widen(extp, 1, rim, widep)

    def fold(n, carry):
        m = pl.multiple_of(n * STEP, STEP)
        ing[pl.ds(m, STEP), :] = g_ref[pl.ds(m, STEP), :].astype(F32) + conv_block(widep, 1, k1t_ref, m, STEP)
        return carry

    lax.fori_loop(0, CELLS // STEP, fold, 0)
    turned_part(trim, 1, k1t_ref, ing)
    for q in range(4):
        part = ing[q * 256 : (q + 1) * 256, :].astype(BF16)
        rounded[q * 16 : (q + 1) * 16] = part.reshape(16, BT, CH)

    def pick(q, carry):
        back_ref[q] = rounded[ids[q]]
        return carry

    lax.fori_loop(0, 2 * PAIRS, pick, 0, unroll=4)
    wait_rows_recv(exth, 2, rssh, rrsh)
    open_slab(recv2, 2, 0, me, rim2)
    widen(exth, 2, rim2, wide2_ref)
    wait_sides_send(send, recv, ss, rs)
    wait_rows_send(ext, 1, rss, rrs)
    wait_sides_send(send2, recv2, ss2, rs2)
    wait_rows_send(exth, 2, rssh, rrsh)
    wait_rows_send(extp, 1, rssp, rrsp)


def mid(flip, ids, x, hidden_grad, grad, k1, k1t):
    dma = pltpu.SemaphoreType.DMA
    return pl.pallas_call(
        mid_kernel,
        name="middle",
        out_shape=(
            jax.ShapeDtypeStruct((2 * PAIRS, BT, CH), BF16),
            jax.ShapeDtypeStruct(((ROWS + 2) * COLS, 3 * CH), BF16),
            jax.ShapeDtypeStruct(((ROWS + 4) * COLS, 3 * CH), BF16),
            jax.ShapeDtypeStruct((CELLS, CH), BF16),
        ),
        in_specs=[SM, SM, VM, VM, VM, VM, VM],
        out_specs=(VM, VM, VM, VM),
        scratch_shapes=[
            pltpu.VMEM((ROWS + 2, COLS, CH), BF16),
            pltpu.VMEM((ROWS + 4, COLS, CH), BF16),
            pltpu.VMEM((ROWS + 2, COLS, CH), BF16),
            pltpu.VMEM((2, 16, CH), BF16),
            pltpu.VMEM((2, 3, 16, CH), BF16),
            pltpu.VMEM((2, 32, CH), BF16),
            pltpu.VMEM((2, 3, 32, CH), BF16),
            pltpu.VMEM((2, 16, CH), F32),
            pltpu.VMEM((2, 1, 16, CH), F32),
            pltpu.VMEM((2, 2, 16, CH), F32),
            pltpu.VMEM((2, 1, 16, CH), F32),
            pltpu.VMEM(((ROWS + 2) * COLS, 3 * CH), BF16),
            pltpu.VMEM((CELLS, CH), F32),
            pltpu.VMEM((BLOCKS, BT, CH), BF16),
            dma((2, 3)), dma((2, 3)), dma((2,)), dma((2,)),
            dma((2, 3)), dma((2, 3)), dma((2,)), dma((2,)), dma((2,)), dma((2,)),
        ],
        compiler_params=params(collective_id=2, has_side_effects=True),
        cost_estimate=pl.CostEstimate(flops=6 * 2**30, bytes_accessed=12 * 2**20, transcendentals=2**18),
    )(flip, ids, x, hidden_grad, grad, k1, k1t)


PART = 3 * CH


def axis_peer(axis, k):
    t, b, tiles, bands = place_in_mesh()
    at = list(spot(t, b))
    at[axis] = lax.rem(at[axis] + k, 4)
    return device_at(*at)


def twin():
    t, b, tiles, bands = place_in_mesh()
    return (t, b + 1 - 2 * lax.rem(b, 2))


def sum_kernel(
    wide1, pg, wide2, g, x_ref, k2_ref, mixed_ref, out_ref,
    acc, send1, recv1, send2, recv2, send3, recv3, recv4,
    s1, r1, s2, r2, s3, r3, s4, r4, s5, r5, s6, r6, s7, r7,
):
    t, b, tiles, bands = place_in_mesh()
    place = spot(t, b)
    core = place[3]
    barrier = pltpu.get_barrier_semaphore()
    pl.semaphore_signal(barrier, inc=1, device_id=twin(), device_id_type=MESH)
    for axis in range(3):
        for k in (1, 2, 3):
            pl.semaphore_signal(barrier, inc=1, device_id=axis_peer(axis, k), device_id_type=MESH)
    pl.semaphore_wait(barrier, 10)

    def axes(o):
        return o, (o + 1) % 3, (o + 2) % 3

    def copy(src, dst, ss, rs, to):
        return pltpu.make_async_remote_copy(
            src_ref=src, dst_ref=dst, send_sem=ss, recv_sem=rs, device_id=to, device_id_type=MESH
        )

    def first(o):
        return copy(send1.at[o], recv1.at[o], s1.at[o], r1.at[o], twin())

    def second(o, k):
        a = axes(o)[0]
        at = pl.ds(pl.multiple_of(lax.rem(place[a] + k, 4) * 192, 64), 192)
        return copy(send2.at[o, at], recv2.at[o, k - 1], s2.at[o, k - 1], r2.at[o, k - 1], axis_peer(a, k))

    def third(o, k):
        a = axes(o)[1]
        at = pl.ds(pl.multiple_of(lax.rem(place[a] + k, 4) * 48, 16), 48)
        return copy(send3.at[o, at], recv3.at[o, k - 1], s3.at[o, k - 1], r3.at[o, k - 1], axis_peer(a, k))

    def fourth(o, k):
        a = axes(o)[2]
        mine = recv4.at[o, place[a]]
        return copy(mine, mine, s4.at[o, k - 1], r4.at[o, k - 1], axis_peer(a, k))

    def fifth(o, k):
        a, c, _ = axes(o)
        rows = out_ref.at[core, o, pl.ds(pl.multiple_of(place[a] * 192 + place[c] * 48, 16), 48)]
        return copy(rows, rows, s5.at[o, k - 1], r5.at[o, k - 1], axis_peer(c, k))

    def sixth(o, k):
        a = axes(o)[0]
        rows = out_ref.at[core, o, pl.ds(pl.multiple_of(place[a] * 192, 64), 192)]
        return copy(rows, rows, s6.at[o, k - 1], r6.at[o, k - 1], axis_peer(a, k))

    def seventh(o):
        return copy(out_ref.at[core, o], out_ref.at[core, o], s7.at[o], r7.at[o], twin())

    for o in range(3):
        acc[1, o] = lax.dot_general(
            wide2[o * 2 * COLS : o * 2 * COLS + CELLS, :], g[...], (((0,), (0,)), ((), ())), preferred_element_type=F32
        )
        acc[0, o] = lax.dot_general(
            wide1[o * COLS : o * COLS + CELLS, :], pg[...], (((0,), (0,)), ((), ())), preferred_element_type=F32
        )
        send1[o] = acc[1 - core, o].astype(BF16)
        first(o).start()
    for o in range(3):
        first(o).wait_recv()
        total = acc[core, o] + recv1[o].astype(F32)
        acc[core, o] = total
        send2[o] = total.astype(BF16)
        for k in (1, 2, 3):
            second(o, k).start()

    def block(n, carry):
        m = pl.multiple_of(n * STEP, STEP)
        mixed_ref[pl.ds(m, STEP), :] = (
            x_ref[pl.ds(m, STEP), :].astype(F32) + conv_block(wide2, 2, k2_ref, m, STEP)
        ).astype(BF16)
        return carry

    lax.fori_loop(0, CELLS // STEP, block, 0)
    for o in range(3):
        a, c, e = axes(o)
        for k in (1, 2, 3):
            second(o, k).wait_recv()
        own = pl.ds(pl.multiple_of(place[a] * 192, 64), 192)
        total = acc[core, o, own, :]
        for k in (1, 2, 3):
            total = total + recv2[o, k - 1].astype(F32)
        acc[core, o, 0:192, :] = total
        send3[o] = total.astype(BF16)
        for k in (1, 2, 3):
            third(o, k).start()
    for o in range(3):
        a, c, e = axes(o)
        for k in (1, 2, 3):
            third(o, k).wait_recv()
        total = acc[core, o, pl.ds(pl.multiple_of(place[c] * 48, 16), 48), :]
        for k in (1, 2, 3):
            total = total + recv3[o, k - 1].astype(F32)
        recv4[o, place[e]] = total.astype(BF16)
        for k in (1, 2, 3):
            fourth(o, k).start()
    for o in range(3):
        a, c, e = axes(o)
        for k in (1, 2, 3):
            fourth(o, k).wait_recv()
        v = [recv4[o, q].astype(F32) for q in range(4)]
        total = ((v[0] + v[1]) + v[2]) + v[3]
        out_ref[core, o, pl.ds(pl.multiple_of(place[a] * 192 + place[c] * 48, 16), 48), :] = total.astype(BF16)
        for k in (1, 2, 3):
            fifth(o, k).start()
    for o in range(3):
        for k in (1, 2, 3):
            fifth(o, k).wait_recv()
        for k in (1, 2, 3):
            sixth(o, k).start()
    for o in range(3):
        for k in (1, 2, 3):
            sixth(o, k).wait_recv()
        seventh(o).start()
    for o in range(3):
        seventh(o).wait_recv()
    for o in range(3):
        first(o).wait_send()
        seventh(o).wait_send()
        for k in (1, 2, 3):
            for step in (second, third, fourth, fifth, sixth):
                step(o, k).wait_send()


def kernel_sums(wide1, pg, wide2, g, x, k2):
    dma = pltpu.SemaphoreType.DMA
    three, nine = [dma((3,))] * 2, [dma((3, 3))] * 2
    return pl.pallas_call(
        sum_kernel,
        name="kernel_sums",
        out_shape=(
            jax.ShapeDtypeStruct((CELLS, CH), BF16),
            jax.ShapeDtypeStruct((2, 3, PART, CH), BF16),
        ),
        in_specs=[VM] * 6,
        out_specs=(VM, VM),
        scratch_shapes=[
            pltpu.VMEM((2, 3, PART, CH), F32),
            pltpu.VMEM((3, PART, CH), BF16),
            pltpu.VMEM((3, PART, CH), BF16),
            pltpu.VMEM((3, PART, CH), BF16),
            pltpu.VMEM((3, 3, 192, CH), BF16),
            pltpu.VMEM((3, 192, CH), BF16),
            pltpu.VMEM((3, 3, 48, CH), BF16),
            pltpu.VMEM((3, 4, 48, CH), BF16),
            *three, *nine, *nine, *nine, *nine, *nine, *three,
        ],
        compiler_params=params(collective_id=3, has_side_effects=True),
        cost_estimate=pl.CostEstimate(flops=20 * 2**30, bytes_accessed=14 * 2**20, transcendentals=0),
    )(wide1, pg, wide2, g, x, k2)


def source_kernel(slot, got_ref, w_ref, ps_ref, sums_ref, out_ref, one_ref, two_ref, rows, wexp):
    for i in range(3):
        one_ref[i] = sums_ref[0, i].astype(F32)
        two_ref[i] = sums_ref[1, i].astype(F32)

    def take(p, carry):
        rows[pl.ds(pl.multiple_of(p * BT, BT), BT), :] = got_ref[slot[p]]
        return carry

    lax.fori_loop(0, PAIRS, take, 0, unroll=4)
    w = w_ref[...]
    ps = ps_ref[...]
    for s in range(SB):
        wexp[s * BL : (s + 1) * BL, :] = w * (ps == s).astype(F32).astype(BF16)
    for m in range(4):
        out_ref[m * 256 : (m + 1) * 256, :] = jnp.dot(
            wexp[m * 256 : (m + 1) * 256, :], rows[...], preferred_element_type=F32
        ).astype(BF16)


def source_side(slot, returned, w_cells, ps_cells, sums):
    return pl.pallas_call(
        source_kernel,
        name="source_grad",
        out_shape=(
            jax.ShapeDtypeStruct((SB * BL, CH), BF16),
            jax.ShapeDtypeStruct((3, PART, CH), F32),
            jax.ShapeDtypeStruct((3, PART, CH), F32),
        ),
        in_specs=[SM, VM, VM, VM, VM],
        out_specs=(VM, VM, VM),
        scratch_shapes=[
            pltpu.VMEM((PAIRS * BT, CH), BF16),
            pltpu.VMEM((SB * BL, PAIRS * BT), BF16),
        ],
        compiler_params=params(),
        cost_estimate=pl.CostEstimate(flops=2 * 2048 * 1024 * 256, bytes_accessed=4 * 2**20, transcendentals=0),
    )(slot, returned, w_cells, ps_cells, sums)


def local(
    source_cells, regrid_weights, pair_target, pair_block, pair_source, flip_codes, kernel_one, kernel_two, out_grad
):
    axes = ("tile", "band")
    me = lax.axis_index(axes)
    target = pair_target[:, 0]
    outgoing, slot = regrid(target, pair_source, regrid_weights, source_cells)
    arrived = lax.all_to_all(outgoing, axes, split_axis=0, concat_axis=0, tiled=True)
    upstream = out_grad[0]
    named = (target * BLOCKS + pair_block)[None, :]
    hidden_grad, k1_back, table = back(flip_codes, named, upstream, kernel_one, kernel_two)
    table = table[:, 0, :]
    order = lax.broadcasted_iota(jnp.int32, table.shape, 1)
    mine = (table // BLOCKS) == me
    first = jnp.min(jnp.where(mine, order, PAIRS), axis=1, keepdims=True)
    last = jnp.max(jnp.where(mine, order, -1), axis=1, keepdims=True)
    block = table % BLOCKS
    id_first = jnp.sum(jnp.where(order == first, block, 0), axis=1) + jnp.where(first[:, 0] == PAIRS, BLOCKS, 0)
    more = last > first
    id_last = jnp.sum(jnp.where((order == last) & more, block, 0), axis=1) + jnp.where(more[:, 0], 0, BLOCKS)
    ids = jnp.stack([id_first, id_last], axis=1).reshape(2 * PAIRS)
    regridded = gather_sum(ids, arrived)
    back_rows, wide1, wide2, pre_grad = mid(
        flip_codes,
        jnp.minimum(ids, BLOCKS - 1),
        regridded.reshape(ROWS, COLS, CH),
        hidden_grad,
        upstream.reshape(CELLS, CH),
        kernel_one.reshape(3, 3 * CH, CH),
        k1_back,
    )
    returned = lax.all_to_all(back_rows, axes, split_axis=0, concat_axis=0, tiled=True)
    mixed, sums = kernel_sums(
        wide1,
        pre_grad,
        wide2,
        upstream.reshape(CELLS, CH),
        regridded.reshape(CELLS, CH),
        kernel_two.reshape(3, PART, CH),
    )
    w_cells = regrid_weights.transpose(2, 0, 1).reshape(BL, PAIRS * BT)
    ps_cells = jnp.repeat(pair_source, BT)[None, :]
    source_grad, one, two = source_side(slot, returned, w_cells, ps_cells, sums)
    return (
        mixed.reshape(1, ROWS, COLS, CH),
        one.reshape(3, 3, CH, CH),
        two.reshape(3, 3, CH, CH),
        source_grad,
    )


def solution(mesh):
    placed = (
        P(("tile", "band"), None),
        P(("tile", "band"), None, None),
        P(("tile", "band"), None),
        P(("tile", "band")),
        P(("tile", "band")),
        P(),
        P(),
        P(),
        P("tile", "band", None, None),
    )
    return jax.shard_map(
        local,
        mesh=mesh,
        in_specs=placed,
        out_specs=(P("tile", "band", None, None), P(), P(), P(("tile", "band"), None)),
        check_vma=False,
    )
```

profile of v0, /device:TPU:1, one launch (start us, length us, event | category | flops | bytes accessed | tf_op | source)
XLA Modules:
  0.0 162.0 jit_solution(14771340709153183098)
XLA Ops:
  0.6 1.4 copy.16.w_ref
  2.0 0.0 copy-start.2
  2.0 0.6 copy-done.2
  2.7 1.0 copy-done.8
  3.7 0.7 copy-done.12
  4.4 7.0 %regrid.1 = (bf16[256,16,256]{2,1,0:T(8,128)(2,1)S(1)}, s32[128]{0:T(128)S(1)}) custom-call(s32[128]{0:T(128)S(1)} %bitcast.30, s32[128]{0:T(128)S(1)} %copy-done.2, bf16[128,16,64]{2,1,0:T(8,128)(2,1)S(1)} %copy.16.w_ref, bf16[1024,256]{1,0:T(8,128)(2,1)S(1)} %copy-done.8), custom_call_target="tpu_custom_call" | custom-call | flops 1073741824 | bytes 6291456 | tf_op jit(solution)/shard_map/regrid/pallas_call | solution.py:62
  11.4 0.0 copy-start.1
  11.4 1.3 copy-done.1
  12.8 11.5 %all-to-all-start = ((bf16[256,16,256]{2,1,0:T(8,128)(2,1)}), bf16[256,16,256]{2,1,0:T(8,128)(2,1)S(1)}, u32[]{:S(2)}, u32[]{:S(2)}) async-start(bf16[256,16,256]{2,1,0:T(8,128)(2,1)} %copy-done.1), calls=%async_computation | async-start | bytes 4194304 | tf_op jit(solution)/shard_map/all_to_all | solution.py:790
  24.3 0.0 copy-done.13
  24.3 0.0 copy-done.23
  24.3 0.0 copy-done.4
  24.3 0.0 copy-done.14
  24.3 0.0 copy-start.6
  24.3 1.3 copy-done.6
  25.6 1.0 copy-done.9
  26.6 33.7 %hidden_adjoint.1 = (f32[1024,256]{1,0:T(8,128)S(1)}, bf16[3,768,256]{2,1,0:T(8,128)(2,1)S(1)}, s32[128,1,128]{2,1,0:T(1,128)S(1)}) custom-call(s32[32]{0:T(128)S(1)} %copy-done.14, s32[1,128]{1,0:T(1,128)S(1)} %add_bitcast_fusion.1.own_ref, bf16[8,128,256]{2,1,0:T(8,128)(2,1)S(1)} %bitcast.27, bf16[3,3,256,256]{3,2,1,0:T(8,128)(2,1)S(1)} %copy-done.4, ...), custom_call_target="tpu_custom_call" | custom-call | flops 6442450944 | bytes 8388608 | tf_op jit(solution)/shard_map/hidden_adjoint/pallas_call | solution.py:431
  60.4 0.0 copy-start.16
  60.4 1.0 copy-done.16
  61.4 1.0 copy-done.18
  62.4 0.1 select_reduce_fusion.3
  62.5 0.2 select_reduce_fusion.2
  62.8 0.1 copy.15
  62.9 0.1 reshape.91.ids
  63.0 0.0 all-to-all-done.got_ref
  63.0 0.0 copy-start.17
  63.1 1.6 gather_sum.1
  64.7 0.0 copy-start.5
  64.7 1.3 copy-done.5
  66.0 25.3 %middle.1 = (bf16[256,16,256]{2,1,0:T(8,128)(2,1)}, bf16[1280,768]{1,0:T(8,128)(2,1)}, bf16[1536,768]{1,0:T(8,128)(2,1)}, bf16[1024,256]{1,0:T(8,128)(2,1)S(1)}) custom-call(s32[32]{0:T(128)S(1)} %copy-done.14, s32[256]{0:T(256)S(1)} %broadcast_minimum_fusion.ids, bf16[8,128,256]{2,1,0:T(8,128)(2,1)S(1)} %bitcast.20, f32[1024,256]{1,0:T(8,128)S(1)} %copy-done.19, ...), custom_call_target="tpu_custom_call" | custom-call | flops 6442450944 | bytes 12582912 | tf_op jit(solution)/shard_map/middle/pallas_call | solution.py:537
  91.2 0.0 copy-start.20
  91.3 0.8 copy-done.20
  92.0 7.6 %all-to-all-start.1 = ((bf16[256,16,256]{2,1,0:T(8,128)(2,1)}), bf16[256,16,256]{2,1,0:T(8,128)(2,1)S(1)}, u32[]{:S(2)}, u32[]{:S(2)}) async-start(bf16[256,16,256]{2,1,0:T(8,128)(2,1)} %get-tuple-element.27), calls=%async_computation.1 | async-start | bytes 4194304 | tf_op jit(solution)/shard_map/all_to_all | solution.py:814
  99.6 0.4 copy.17
  100.1 0.2 copy.18.w_ref
  100.3 0.1 broadcast_in_dim.26
  100.4 0.1 broadcast_in_dim_reshape.3.ps_ref
  100.5 0.0 copy-start.7
  100.5 1.3 copy-done.7
  101.7 1.0 copy-done.11
  102.8 1.5 copy-done.15
  104.3 1.0 copy-done.21
  105.4 49.5 %kernel_sums.1 = (bf16[1024,256]{1,0:T(8,128)(2,1)S(1)}, bf16[2,3,768,256]{3,2,1,0:T(8,128)(2,1)}) custom-call(bf16[1280,768]{1,0:T(8,128)(2,1)S(1)} %copy-done.15, bf16[1024,256]{1,0:T(8,128)(2,1)S(1)} %copy-done.21, bf16[1536,768]{1,0:T(8,128)(2,1)} %get-tuple-element.24.wide2, bf16[1024,256]{1,0:T(8,128)(2,1)S(1)} %bitcast.29, ...), custom_call_target="tpu_custom_call" | custom-call | flops 21474836480 | bytes 14680064 | tf_op jit(solution)/shard_map/kernel_sums/pallas_call | solution.py:718
  154.9 0.0 all-to-all-done.1.got_ref
  154.9 0.0 copy-start
  154.9 1.7 %copy-done = bf16[2,3,768,256]{3,2,1,0:T(8,128)(2,1)S(1)} copy-done((bf16[2,3,768,256]{3,2,1,0:T(8,128)(2,1)S(1)}, bf16[2,3,768,256]{3,2,1,0:T(8,128)(2,1)}, u32[]{:S(2)}) %copy-start) | copy-done | bytes 2359320
  156.5 4.7 %source_grad.1 = (bf16[1024,256]{1,0:T(8,128)(2,1)}, f32[3,768,256]{2,1,0:T(8,128)}, f32[3,768,256]{2,1,0:T(8,128)}) custom-call(s32[128]{0:T(128)S(1)} %get-tuple-element.26.slot, bf16[256,16,256]{2,1,0:T(8,128)(2,1)S(1)} %all-to-all-done.1.got_ref, bf16[64,2048]{1,0:T(8,128)(2,1)S(1)} %copy.18.w_ref, s32[1,2048]{1,0:T(1,128)S(1)} %broadcast_in_dim_reshape.3.ps_ref, ...), custom_call_target="tpu_custom_call" | custom-call | flops 1073741824 | bytes 4194304 | tf_op jit(solution)/shard_map/source_grad/pallas_call | solution.py:764
  161.2 0.8 copy.20
  (25 shorter events, 0.1 us)
Async XLA Ops:
  2.0 0.7 copy-start.2
  2.7 1.0 copy-start.8
  3.7 0.7 copy-start.12
  11.4 1.3 copy-start.1
  12.7 11.5 %copy-start.13 = (s32[128,1]{0,1:T(1,128)S(1)}, s32[128,1]{0,1:T(1,128)}, u32[]{:S(2)}) copy-start(s32[128,1]{0,1:T(1,128)} %param.11) | copy-start | bytes 1540
  12.7 11.5 %copy-start.23 = (s32[128]{0:T(128)S(1)}, s32[128]{0:T(128)}, u32[]{:S(2)}) copy-start(s32[128]{0:T(128)} %param.12) | copy-start | bytes 1540
  12.7 11.6 %copy-start.4 = (bf16[3,3,256,256]{3,2,1,0:T(8,128)(2,1)S(1)}, bf16[3,3,256,256]{3,2,1,0:T(8,128)(2,1)}, u32[]{:S(2)}) copy-start(bf16[3,3,256,256]{3,2,1,0:T(8,128)(2,1)} %k1_ref.1) | copy-start | bytes 3538948
  12.7 11.6 %copy-start.14 = (s32[32]{0:T(128)S(1)}, s32[32]{0:T(128)}, u32[]{:S(2)}) copy-start(s32[32]{0:T(128)} %flip.3) | copy-start | bytes 388
  12.8 50.3 %all-to-all-start = ((bf16[256,16,256]{2,1,0:T(8,128)(2,1)}), bf16[256,16,256]{2,1,0:T(8,128)(2,1)S(1)}, u32[]{:S(2)}, u32[]{:S(2)}) async-start(bf16[256,16,256]{2,1,0:T(8,128)(2,1)} %copy-done.1), calls=%async_computation | async-start | bytes 4194304 | tf_op jit(solution)/shard_map/all_to_all | solution.py:790
  24.3 1.3 copy-start.6
  25.6 1.0 copy-start.9
  60.4 1.0 copy-start.16
  61.4 1.0 copy-start.18
  62.4 2.3 %copy-start.10 = (bf16[1,8,128,256]{3,2,1,0:T(8,128)(2,1)S(1)}, bf16[1,8,128,256]{3,2,1,0:T(8,128)(2,1)}, u32[]{:S(2)}) copy-start(bf16[1,8,128,256]{3,2,1,0:T(8,128)(2,1)} %param.17) | copy-start | bytes 1572868
  63.0 1.7 %copy-start.17 = (bf16[3,768,256]{2,1,0:T(8,128)(2,1)S(1)}, bf16[3,768,256]{2,1,0:T(8,128)(2,1)}, u32[]{:S(2)}) copy-start(bf16[3,768,256]{2,1,0:T(8,128)(2,1)} %copy-done.16) | copy-start | bytes 3538948
  63.0 1.7 %copy-start.19 = (f32[1024,256]{1,0:T(8,128)S(1)}, f32[1024,256]{1,0:T(8,128)}, u32[]{:S(2)}) copy-start(f32[1024,256]{1,0:T(8,128)} %copy-done.18) | copy-start | bytes 3145732
  64.7 1.3 copy-start.5
  91.2 0.8 copy-start.20
  92.0 7.6 %copy-start.22 = (bf16[128,16,64]{0,2,1:T(8,128)(2,1)S(1)}, bf16[128,16,64]{0,2,1:T(8,128)(2,1)}, u32[]{:S(2)}) copy-start(bf16[128,16,64]{0,2,1:T(8,128)(2,1)} %param.10) | copy-start | bytes 786436
  92.0 8.2 %copy-start.3 = (s32[128]{0:T(128)S(1)}, s32[128]{0:T(128)}, u32[]{:S(2)}) copy-start(s32[128]{0:T(128)} %psrc.1) | copy-start | bytes 1540
  92.0 62.8 %all-to-all-start.1 = ((bf16[256,16,256]{2,1,0:T(8,128)(2,1)}), bf16[256,16,256]{2,1,0:T(8,128)(2,1)S(1)}, u32[]{:S(2)}, u32[]{:S(2)}) async-start(bf16[256,16,256]{2,1,0:T(8,128)(2,1)} %get-tuple-element.27), calls=%async_computation.1 | async-start | bytes 4194304 | tf_op jit(solution)/shard_map/all_to_all | solution.py:814
  100.5 1.3 copy-start.7
  101.7 1.0 copy-start.11
  102.8 1.5 copy-start.15
  104.3 1.0 copy-start.21
  154.9 1.7 %copy-start = (bf16[2,3,768,256]{3,2,1,0:T(8,128)(2,1)S(1)}, bf16[2,3,768,256]{3,2,1,0:T(8,128)(2,1)}, u32[]{:S(2)}) copy-start(bf16[2,3,768,256]{3,2,1,0:T(8,128)(2,1)} %get-tuple-element.28.sums_ref) | copy-start | bytes 7077892
where the time goes:
time: 163 us; the launch traced here: 162 us
  Pallas kernels  122 us (75%)
  local copies, waits for them, and re-layouts  19.8 us (12%)
  starting transfers between devices  19.1 us (12%)
    pallas_call x1, Pallas kernels, kernel_sums(): pl.pallas_call(sum_kernel, name='kernel_sums', out_shape=(jax.ShapeDtypeS...  49.5 us
    pallas_call x1, Pallas kernels, back(): pl.pallas_call(back_kernel, name='hidden_adjoint', out_shape=(jax.ShapeDt...  33.7 us
    pallas_call x1, Pallas kernels, mid(): pl.pallas_call(mid_kernel, name='middle', out_shape=(jax.ShapeDtypeStruct...  25.3 us
    unnamed x50, local copies, waits for them, and re-layouts  18.8 us
    all_to_all x1, starting transfers between devices, local(): lax.all_to_all(outgoing, axes, split_axis=0, concat_axis=0, tiled=True)  11.5 us
    all_to_all x1, starting transfers between devices, local(): lax.all_to_all(back_rows, axes, split_axis=0, concat_axis=0, tiled=True)  7.56 us
    pallas_call x1, Pallas kernels, regrid(): pl.pallas_call(regrid_kernel, name='regrid', out_shape=(jax.ShapeDtypeStr...  7.04 us
    pallas_call x1, Pallas kernels, source_side(): pl.pallas_call(source_kernel, name='source_grad', out_shape=(jax.ShapeDty...  4.66 us
  transfers between devices with their start and end apart: 2, of which 0 were waited for; matrix products, arithmetic and copies ran while one was open for 1% of the time, Pallas kernels for 51%

commit v1 on v0

--- a/solution.py
+++ b/solution.py
@@ -36,7 +36,7 @@
         t = tgt[p]
         r = cnt[t]
         cnt[t] = r + 1
-        slot_ref[p] = jnp.minimum(2 * t + r, 2 * PAIRS - 1)
+        slot_ref[p] = jnp.minimum(r, 1) * PAIRS + t
         return c
 
     lax.fori_loop(0, PAIRS, rank, 0)
@@ -55,7 +55,9 @@
     for m in range(4):
         part = jnp.dot(wexp[m * 512 : (m + 1) * 512, :], src_ref[...], preferred_element_type=F32).astype(BF16)
         for q in range(32):
-            out_ref[slot_ref[m * 32 + q]] = part[q * BT : (q + 1) * BT]
+            at = slot_ref[m * 32 + q]
+            for h in (0, 1):
+                out_ref[h, at] = part[q * BT : (q + 1) * BT, h * 128 : (h + 1) * 128]
 
 
 def regrid(tgt, psrc, weights, source):
@@ -63,7 +65,7 @@
         regrid_kernel,
         name="regrid",
         out_shape=(
-            jax.ShapeDtypeStruct((2 * PAIRS, BT, CH), BF16),
+            jax.ShapeDtypeStruct((2, 2 * PAIRS, BT, 128), BF16),
             jax.ShapeDtypeStruct((PAIRS,), jnp.int32),
         ),
         in_specs=[SM, SM, VM, VM],
@@ -83,7 +85,8 @@
 
     def add(q, c):
         k = ids[q]
-        acc[k] += got_ref[q].astype(F32)
+        for h in (0, 1):
+            acc[k, :, h * 128 : (h + 1) * 128] += got_ref[h, q].astype(F32)
         return c
 
     lax.fori_loop(0, 2 * PAIRS, add, 0, unroll=8)
@@ -337,6 +340,132 @@
     return (y * 8 + lax.div(z, 2) * 4 + x, lax.rem(z, 2) * 2 + core)
 
 
+WORLD = (4, 4, 2, 4, 2, 2, BT, 128)
+UNITS = [(hs, c) for c in (0, 1) for hs in range(4)]
+
+
+def axis_peer(axis, k):
+    t, b, tiles, bands = place_in_mesh()
+    at = list(spot(t, b))
+    at[axis] = lax.rem(at[axis] + k, 4)
+    return device_at(*at)
+
+
+def twin():
+    t, b, tiles, bands = place_in_mesh()
+    return (t, b + 1 - 2 * lax.rem(b, 2))
+
+
+def greet_axes():
+    barrier = pltpu.get_barrier_semaphore()
+    pl.semaphore_signal(barrier, inc=1, device_id=twin(), device_id_type=MESH)
+    for axis in range(3):
+        for k in (1, 2, 3):
+            pl.semaphore_signal(barrier, inc=1, device_id=axis_peer(axis, k), device_id_type=MESH)
+
+
+AXIS_PEERS = 10
+
+
+def along(ref, unit, axis, v):
+    hs, c = UNITS[unit]
+    if axis == 0:
+        return ref.at[hs, :, :, v, :, c]
+    if axis == 1:
+        return ref.at[hs, v, :, :, :, c]
+    return ref.at[hs, :, lax.div(v, 2), :, lax.rem(v, 2), c]
+
+
+def remote(src, dst, ss, rs, to):
+    return pltpu.make_async_remote_copy(
+        src_ref=src, dst_ref=dst, send_sem=ss, recv_sem=rs, device_id=to, device_id_type=MESH
+    )
+
+
+class Swap:
+    def __init__(self, bufs, sems):
+        self.bufs, self.sems = bufs, sems
+        t, b, tiles, bands = place_in_mesh()
+        self.place = spot(t, b)
+
+    def core_copy(self, hs):
+        me = self.place[3]
+        src, dst = self.bufs[0], self.bufs[1]
+        ss, rs = self.sems[0], self.sems[1]
+        return remote(
+            src.at[hs, :, :, :, :, 1 - me], dst.at[hs, :, :, :, :, me], ss.at[hs], rs.at[hs], twin()
+        )
+
+    def core_own(self, hs):
+        me = self.place[3]
+        src, dst = self.bufs[0], self.bufs[1]
+        return pltpu.make_async_copy(src.at[hs, :, :, :, :, me], dst.at[hs, :, :, :, :, me], self.sems[2].at[hs])
+
+    def core_start(self, hs):
+        self.core_copy(hs).start()
+        self.core_own(hs).start()
+
+    def core_wait(self, hs):
+        self.core_copy(hs).wait_recv()
+        self.core_own(hs).wait()
+
+    def hop(self, stage, u, k):
+        axis = (u + stage) % 3
+        me = self.place[axis]
+        src, dst = self.bufs[1 + stage], self.bufs[2 + stage]
+        return remote(
+            along(src, u, axis, lax.rem(me + k, 4)), along(dst, u, axis, me),
+            self.sems[3].at[stage, u, k - 1], self.sems[4].at[stage, u, k - 1], axis_peer(axis, k),
+        )
+
+    def own(self, stage, u):
+        axis = (u + stage) % 3
+        me = self.place[axis]
+        src, dst = self.bufs[1 + stage], self.bufs[2 + stage]
+        return pltpu.make_async_copy(along(src, u, axis, me), along(dst, u, axis, me), self.sems[5].at[stage, u])
+
+    def start(self, stage, u):
+        for k in (2, 1, 3):
+            self.hop(stage, u, k).start()
+        self.own(stage, u).start()
+
+    def wait(self, stage, u):
+        for k in (1, 2, 3):
+            self.hop(stage, u, k).wait_recv()
+        self.own(stage, u).wait()
+
+    def first_stage(self):
+        done = set()
+        for u in range(8):
+            hs = UNITS[u][0]
+            if hs not in done:
+                self.core_wait(hs)
+                done.add(hs)
+            self.start(0, u)
+
+    def next_stage(self, stage):
+        for u in range(8):
+            self.wait(stage - 1, u)
+            self.start(stage, u)
+
+    def last_wait(self):
+        for u in range(8):
+            self.wait(2, u)
+
+    def drain(self):
+        for hs in range(4):
+            self.core_copy(hs).wait_send()
+        for stage in range(3):
+            for u in range(8):
+                for k in (1, 2, 3):
+                    self.hop(stage, u, k).wait_send()
+
+
+def swap_sems():
+    dma = pltpu.SemaphoreType.DMA
+    return [dma((4,)), dma((4,)), dma((4,)), dma((3, 8, 3)), dma((3, 8, 3)), dma((3, 8))]
+
+
 def table_peer(stage, k):
     t, b, tiles, bands = place_in_mesh()
     x, y, z, core = spot(t, b)
@@ -382,10 +511,11 @@
 
 
 def back_kernel(
-    flip, own_ref, g_ref, k1_ref, k2_ref, hg_ref, k1t_ref, tab,
-    ext, send, recv, tmp, rim, trim, wide, k2t, ss, rs, rss, rrs, tss, trs,
+    flip, own_ref, g_ref, k1_ref, k2_ref, outgoing, hg_ref, k1t_ref, tab, arrived,
+    ext, send, recv, tmp, rim, trim, wide, k2t, b1, b2, b3, ss, rs, rss, rrs, tss, trs, *sems,
 ):
     d = 2
+    swap = Swap((outgoing, b1, b2, b3, arrived), sems)
     t, b, tiles, bands = place_in_mesh()
     tab[t * 4 + b] = own_ref[...]
     me, before, after = flags(flip)
@@ -394,23 +524,30 @@
     clear_edges(ext, d)
     clear_groups(recv)
     greet_table()
-    greet(sum(TABLE_PEERS))
+    greet_axes()
+    greet(sum(TABLE_PEERS) + AXIS_PEERS)
+    for hs in range(4):
+        swap.core_start(hs)
     table_start(tab, tss, trs, 0)
     start_sides(send, recv, ss, rs)
     start_rows(ext, d, rss, rrs)
+    table_wait(tab, tss, trs, 0)
+    table_start(tab, tss, trs, 1)
+    swap.first_stage()
     for i in range(3):
         for j in range(3):
             k2t[i, j * CH : (j + 1) * CH, :] = k2_ref[2 - i, 2 - j].T
             k1t_ref[i, j * CH : (j + 1) * CH, :] = k1_ref[2 - i, 2 - j].T
-    table_wait(tab, tss, trs, 0)
-    table_start(tab, tss, trs, 1)
+    table_wait(tab, tss, trs, 1)
+    table_start(tab, tss, trs, 2)
     wait_sides_recv(send, recv, ss, rs)
     wait_rows_recv(ext, d, rss, rrs)
     open_slab(recv, d, 0, me, rim)
     split_rim(rim, d, me, before, after, trim)
     widen(ext, d, rim, wide)
-    table_wait(tab, tss, trs, 1)
-    table_start(tab, tss, trs, 2)
+    table_wait(tab, tss, trs, 2)
+    table_start(tab, tss, trs, 3)
+    swap.next_stage(1)
 
     def block(n, carry):
         m = pl.multiple_of(n * STEP, STEP)
@@ -418,15 +555,16 @@
         return carry
 
     lax.fori_loop(0, CELLS // STEP, block, 0)
-    table_wait(tab, tss, trs, 2)
-    table_start(tab, tss, trs, 3)
     turned_part(trim, d, k2t, hg_ref)
+    swap.next_stage(2)
     table_wait(tab, tss, trs, 3)
     wait_sides_send(send, recv, ss, rs)
     wait_rows_send(ext, d, rss, rrs)
-
-
-def back(flip, own, grad, k1, k2):
+    swap.last_wait()
+    swap.drain()
+
+
+def back(flip, own, grad, k1, k2, outgoing):
     d = 2
     return pl.pallas_call(
         back_kernel,
@@ -435,9 +573,10 @@
             jax.ShapeDtypeStruct((CELLS, CH), F32),
             jax.ShapeDtypeStruct((3, 3 * CH, CH), BF16),
             jax.ShapeDtypeStruct((PAIRS, 1, PAIRS), jnp.int32),
+            jax.ShapeDtypeStruct(WORLD, BF16),
         ),
-        in_specs=[SM, VM, VM, VM, VM],
-        out_specs=(VM, VM, VM),
+        in_specs=[SM, VM, VM, VM, VM, VM],
+        out_specs=(VM, VM, VM, VM),
         scratch_shapes=[
             pltpu.VMEM((ROWS + 2 * d, COLS, CH), BF16),
             pltpu.VMEM((2, 16, CH), BF16),
@@ -447,24 +586,33 @@
             pltpu.VMEM((2, d, 16, CH), F32),
             pltpu.VMEM(((ROWS + 2 * d) * COLS, 3 * CH), BF16),
             pltpu.VMEM((3, 3 * CH, CH), BF16),
+            pltpu.VMEM(WORLD, BF16),
+            pltpu.VMEM(WORLD, BF16),
+            pltpu.VMEM(WORLD, BF16),
             pltpu.SemaphoreType.DMA((2, 3)),
             pltpu.SemaphoreType.DMA((2, 3)),
             pltpu.SemaphoreType.DMA((2,)),
             pltpu.SemaphoreType.DMA((2,)),
             pltpu.SemaphoreType.DMA((4, 3)),
             pltpu.SemaphoreType.DMA((4, 3)),
+            *swap_sems(),
         ],
         compiler_params=params(collective_id=1, has_side_effects=True),
         cost_estimate=pl.CostEstimate(flops=6 * 2**30, bytes_accessed=8 * 2**20, transcendentals=0),
-    )(flip, own, grad, k1, k2)
+    )(flip, own, grad, k1, k2, outgoing)
 
 
 def mid_kernel(
-    flip, ids, x_ref, hg_ref, g_ref, k1_ref, k1t_ref,
-    back_ref, wide1_ref, wide2_ref, pg_ref,
-    ext, exth, extp, send, recv, send2, recv2, tmp, rim, rim2, trim, widep, ing, rounded,
+    flip, ids, slot, x_ref, hg_ref, g_ref, k1_ref, k1t_ref, k2_ref, w_ref, ps_ref,
+    mixed_ref, out_ref, source_ref,
+    ext, exth, extp, send, recv, send2, recv2, tmp, rim, rim2, trim, wide1_ref, wide2_ref, widep, pg_ref, ing, rounded,
+    b0, b1, b2, b3, b4, rows, wexp,
+    acc, send1, recv1, sent2, got2, sent3, got3, got4,
     ss, rs, rss, rrs, ss2, rs2, rssh, rrsh, rssp, rrsp,
+    s1, r1, s2, r2, s3, r3, s4, r4, s5, r5, s6, r6, s7, r7, *sems,
 ):
+    swap = Swap((b0, b1, b2, b3, b4), sems)
+    sums = Sums(out_ref, acc, send1, recv1, sent2, got2, sent3, got3, got4, (s1, r1, s2, r2, s3, r3, s4, r4, s5, r5, s6, r6, s7, r7))
     me, before, after = flags(flip)
     ext[pl.ds(1, ROWS)] = x_ref[...]
     make_slab(ext, 1, send, 0, me, tmp)
@@ -473,7 +621,8 @@
     clear_edges(extp, 1)
     clear_groups(recv)
     clear_groups(recv2)
-    greet()
+    greet_axes()
+    greet(AXIS_PEERS)
     start_sides(send, recv, ss, rs)
     start_rows(ext, 1, rss, rrs)
     wait_sides_recv(send, recv, ss, rs)
@@ -517,34 +666,98 @@
         part = ing[q * 256 : (q + 1) * 256, :].astype(BF16)
         rounded[q * 16 : (q + 1) * 16] = part.reshape(16, BT, CH)
 
-    def pick(q, carry):
-        back_ref[q] = rounded[ids[q]]
-        return carry
-
-    lax.fori_loop(0, 2 * PAIRS, pick, 0, unroll=4)
+    for half in (0, 1):
+
+        def pick(q, carry):
+            block = rounded[ids[half * PAIRS + q]]
+            y, zh, x = lax.div(q, 32), lax.rem(lax.div(q, 16), 2), lax.rem(lax.div(q, 4), 4)
+            zl, c = lax.rem(lax.div(q, 2), 2), lax.rem(q, 2)
+            b0[half, y, zh, x, zl, c] = block[:, 0:128]
+            b0[2 + half, y, zh, x, zl, c] = block[:, 128:256]
+            return carry
+
+        lax.fori_loop(0, PAIRS, pick, 0, unroll=4)
+        swap.core_start(half)
+        swap.core_start(2 + half)
     wait_rows_recv(exth, 2, rssh, rrsh)
     open_slab(recv2, 2, 0, me, rim2)
     widen(exth, 2, rim2, wide2_ref)
+    swap.first_stage()
+    for o in range(3):
+        acc[1, o] = lax.dot_general(
+            wide2_ref[o * 2 * COLS : o * 2 * COLS + CELLS, :],
+            g_ref[...],
+            (((0,), (0,)), ((), ())),
+            preferred_element_type=F32,
+        )
+        acc[0, o] = lax.dot_general(
+            wide1_ref[o * COLS : o * COLS + CELLS, :],
+            pg_ref[...],
+            (((0,), (0,)), ((), ())),
+            preferred_element_type=F32,
+        )
+        sums.start(o)
+    sums.to_second()
+    swap.next_stage(1)
+
+    def block(n, carry):
+        m = pl.multiple_of(n * STEP, STEP)
+        mixed_ref[pl.ds(m, STEP), :] = (
+            x_ref[pl.ds(m // COLS, STEP // COLS)].reshape(STEP, CH).astype(F32)
+            + conv_block(wide2_ref, 2, k2_ref, m, STEP)
+        ).astype(BF16)
+        return carry
+
+    lax.fori_loop(0, CELLS // STEP, block, 0)
+    w = w_ref[...]
+    ps = ps_ref[...]
+    for n in range(SB):
+        wexp[n * BL : (n + 1) * BL, :] = w * (ps == n).astype(F32).astype(BF16)
+    sums.to_third()
+    swap.next_stage(2)
+    sums.to_fourth()
+    sums.to_fifth()
+    sums.to_sixth()
+    swap.last_wait()
+
+    def take(p, carry):
+        q = slot[p]
+        half, t = lax.div(q, PAIRS), lax.rem(q, PAIRS)
+        y, zh, x = lax.div(t, 32), lax.rem(lax.div(t, 16), 2), lax.rem(lax.div(t, 4), 4)
+        zl, c = lax.rem(lax.div(t, 2), 2), lax.rem(t, 2)
+        at = pl.ds(pl.multiple_of(p * BT, BT), BT)
+        rows[at, 0:128] = b4[half, y, zh, x, zl, c]
+        rows[at, 128:256] = b4[2 + half, y, zh, x, zl, c]
+        return carry
+
+    lax.fori_loop(0, PAIRS, take, 0, unroll=4)
+    for m in range(4):
+        source_ref[m * 256 : (m + 1) * 256, :] = jnp.dot(
+            wexp[m * 256 : (m + 1) * 256, :], rows[...], preferred_element_type=F32
+        ).astype(BF16)
+    sums.to_seventh()
+    sums.finish()
     wait_sides_send(send, recv, ss, rs)
     wait_rows_send(ext, 1, rss, rrs)
     wait_sides_send(send2, recv2, ss2, rs2)
     wait_rows_send(exth, 2, rssh, rrsh)
     wait_rows_send(extp, 1, rssp, rrsp)
-
-
-def mid(flip, ids, x, hidden_grad, grad, k1, k1t):
+    swap.drain()
+
+
+def mid(flip, ids, slot, x, hidden_grad, grad, k1, k1t, k2, w_cells, ps_cells):
     dma = pltpu.SemaphoreType.DMA
+    three, nine = [dma((3,))] * 2, [dma((3, 3))] * 2
     return pl.pallas_call(
         mid_kernel,
         name="middle",
         out_shape=(
-            jax.ShapeDtypeStruct((2 * PAIRS, BT, CH), BF16),
-            jax.ShapeDtypeStruct(((ROWS + 2) * COLS, 3 * CH), BF16),
-            jax.ShapeDtypeStruct(((ROWS + 4) * COLS, 3 * CH), BF16),
             jax.ShapeDtypeStruct((CELLS, CH), BF16),
+            jax.ShapeDtypeStruct((2, 3, PART, CH), BF16),
+            jax.ShapeDtypeStruct((SB * BL, CH), BF16),
         ),
-        in_specs=[SM, SM, VM, VM, VM, VM, VM],
-        out_specs=(VM, VM, VM, VM),
+        in_specs=[SM, SM, SM] + [VM] * 8,
+        out_specs=(VM, VM, VM),
         scratch_shapes=[
             pltpu.VMEM((ROWS + 2, COLS, CH), BF16),
             pltpu.VMEM((ROWS + 4, COLS, CH), BF16),
@@ -558,173 +771,14 @@
             pltpu.VMEM((2, 2, 16, CH), F32),
             pltpu.VMEM((2, 1, 16, CH), F32),
             pltpu.VMEM(((ROWS + 2) * COLS, 3 * CH), BF16),
+            pltpu.VMEM(((ROWS + 4) * COLS, 3 * CH), BF16),
+            pltpu.VMEM(((ROWS + 2) * COLS, 3 * CH), BF16),
+            pltpu.VMEM((CELLS, CH), BF16),
             pltpu.VMEM((CELLS, CH), F32),
             pltpu.VMEM((BLOCKS, BT, CH), BF16),
-            dma((2, 3)), dma((2, 3)), dma((2,)), dma((2,)),
-            dma((2, 3)), dma((2, 3)), dma((2,)), dma((2,)), dma((2,)), dma((2,)),
-        ],
-        compiler_params=params(collective_id=2, has_side_effects=True),
-        cost_estimate=pl.CostEstimate(flops=6 * 2**30, bytes_accessed=12 * 2**20, transcendentals=2**18),
-    )(flip, ids, x, hidden_grad, grad, k1, k1t)
-
-
-PART = 3 * CH
-
-
-def axis_peer(axis, k):
-    t, b, tiles, bands = place_in_mesh()
-    at = list(spot(t, b))
-    at[axis] = lax.rem(at[axis] + k, 4)
-    return device_at(*at)
-
-
-def twin():
-    t, b, tiles, bands = place_in_mesh()
-    return (t, b + 1 - 2 * lax.rem(b, 2))
-
-
-def sum_kernel(
-    wide1, pg, wide2, g, x_ref, k2_ref, mixed_ref, out_ref,
-    acc, send1, recv1, send2, recv2, send3, recv3, recv4,
-    s1, r1, s2, r2, s3, r3, s4, r4, s5, r5, s6, r6, s7, r7,
-):
-    t, b, tiles, bands = place_in_mesh()
-    place = spot(t, b)
-    core = place[3]
-    barrier = pltpu.get_barrier_semaphore()
-    pl.semaphore_signal(barrier, inc=1, device_id=twin(), device_id_type=MESH)
-    for axis in range(3):
-        for k in (1, 2, 3):
-            pl.semaphore_signal(barrier, inc=1, device_id=axis_peer(axis, k), device_id_type=MESH)
-    pl.semaphore_wait(barrier, 10)
-
-    def axes(o):
-        return o, (o + 1) % 3, (o + 2) % 3
-
-    def copy(src, dst, ss, rs, to):
-        return pltpu.make_async_remote_copy(
-            src_ref=src, dst_ref=dst, send_sem=ss, recv_sem=rs, device_id=to, device_id_type=MESH
-        )
-
-    def first(o):
-        return copy(send1.at[o], recv1.at[o], s1.at[o], r1.at[o], twin())
-
-    def second(o, k):
-        a = axes(o)[0]
-        at = pl.ds(pl.multiple_of(lax.rem(place[a] + k, 4) * 192, 64), 192)
-        return copy(send2.at[o, at], recv2.at[o, k - 1], s2.at[o, k - 1], r2.at[o, k - 1], axis_peer(a, k))
-
-    def third(o, k):
-        a = axes(o)[1]
-        at = pl.ds(pl.multiple_of(lax.rem(place[a] + k, 4) * 48, 16), 48)
-        return copy(send3.at[o, at], recv3.at[o, k - 1], s3.at[o, k - 1], r3.at[o, k - 1], axis_peer(a, k))
-
-    def fourth(o, k):
-        a = axes(o)[2]
-        mine = recv4.at[o, place[a]]
-        return copy(mine, mine, s4.at[o, k - 1], r4.at[o, k - 1], axis_peer(a, k))
-
-    def fifth(o, k):
-        a, c, _ = axes(o)
-        rows = out_ref.at[core, o, pl.ds(pl.multiple_of(place[a] * 192 + place[c] * 48, 16), 48)]
-        return copy(rows, rows, s5.at[o, k - 1], r5.at[o, k - 1], axis_peer(c, k))
-
-    def sixth(o, k):
-        a = axes(o)[0]
-        rows = out_ref.at[core, o, pl.ds(pl.multiple_of(place[a] * 192, 64), 192)]
-        return copy(rows, rows, s6.at[o, k - 1], r6.at[o, k - 1], axis_peer(a, k))
-
-    def seventh(o):
-        return copy(out_ref.at[core, o], out_ref.at[core, o], s7.at[o], r7.at[o], twin())
-
-    for o in range(3):
-        acc[1, o] = lax.dot_general(
-            wide2[o * 2 * COLS : o * 2 * COLS + CELLS, :], g[...], (((0,), (0,)), ((), ())), preferred_element_type=F32
-        )
-        acc[0, o] = lax.dot_general(
-            wide1[o * COLS : o * COLS + CELLS, :], pg[...], (((0,), (0,)), ((), ())), preferred_element_type=F32
-        )
-        send1[o] = acc[1 - core, o].astype(BF16)
-        first(o).start()
-    for o in range(3):
-        first(o).wait_recv()
-        total = acc[core, o] + recv1[o].astype(F32)
-        acc[core, o] = total
-        send2[o] = total.astype(BF16)
-        for k in (1, 2, 3):
-            second(o, k).start()
-
-    def block(n, carry):
-        m = pl.multiple_of(n * STEP, STEP)
-        mixed_ref[pl.ds(m, STEP), :] = (
-            x_ref[pl.ds(m, STEP), :].astype(F32) + conv_block(wide2, 2, k2_ref, m, STEP)
-        ).astype(BF16)
-        return carry
-
-    lax.fori_loop(0, CELLS // STEP, block, 0)
-    for o in range(3):
-        a, c, e = axes(o)
-        for k in (1, 2, 3):
-            second(o, k).wait_recv()
-        own = pl.ds(pl.multiple_of(place[a] * 192, 64), 192)
-        total = acc[core, o, own, :]
-        for k in (1, 2, 3):
-            total = total + recv2[o, k - 1].astype(F32)
-        acc[core, o, 0:192, :] = total
-        send3[o] = total.astype(BF16)
-        for k in (1, 2, 3):
-            third(o, k).start()
-    for o in range(3):
-        a, c, e = axes(o)
-        for k in (1, 2, 3):
-            third(o, k).wait_recv()
-        total = acc[core, o, pl.ds(pl.multiple_of(place[c] * 48, 16), 48), :]
-        for k in (1, 2, 3):
-            total = total + recv3[o, k - 1].astype(F32)
-        recv4[o, place[e]] = total.astype(BF16)
-        for k in (1, 2, 3):
-            fourth(o, k).start()
-    for o in range(3):
-        a, c, e = axes(o)
-        for k in (1, 2, 3):
-            fourth(o, k).wait_recv()
-        v = [recv4[o, q].astype(F32) for q in range(4)]
-        total = ((v[0] + v[1]) + v[2]) + v[3]
-        out_ref[core, o, pl.ds(pl.multiple_of(place[a] * 192 + place[c] * 48, 16), 48), :] = total.astype(BF16)
-        for k in (1, 2, 3):
-            fifth(o, k).start()
-    for o in range(3):
-        for k in (1, 2, 3):
-            fifth(o, k).wait_recv()
-        for k in (1, 2, 3):
-            sixth(o, k).start()
-    for o in range(3):
-        for k in (1, 2, 3):
-            sixth(o, k).wait_recv()
-        seventh(o).start()
-    for o in range(3):
-        seventh(o).wait_recv()
-    for o in range(3):
-        first(o).wait_send()
-        seventh(o).wait_send()
-        for k in (1, 2, 3):
-            for step in (second, third, fourth, fifth, sixth):
-                step(o, k).wait_send()
-
-
-def kernel_sums(wide1, pg, wide2, g, x, k2):
-    dma = pltpu.SemaphoreType.DMA
-    three, nine = [dma((3,))] * 2, [dma((3, 3))] * 2
-    return pl.pallas_call(
-        sum_kernel,
-        name="kernel_sums",
-        out_shape=(
-            jax.ShapeDtypeStruct((CELLS, CH), BF16),
-            jax.ShapeDtypeStruct((2, 3, PART, CH), BF16),
-        ),
-        in_specs=[VM] * 6,
-        out_specs=(VM, VM),
-        scratch_shapes=[
+            *[pltpu.VMEM(WORLD, BF16)] * 5,
+            pltpu.VMEM((PAIRS * BT, CH), BF16),
+            pltpu.VMEM((SB * BL, PAIRS * BT), BF16),
             pltpu.VMEM((2, 3, PART, CH), F32),
             pltpu.VMEM((3, PART, CH), BF16),
             pltpu.VMEM((3, PART, CH), BF16),
@@ -733,51 +787,142 @@
             pltpu.VMEM((3, 192, CH), BF16),
             pltpu.VMEM((3, 3, 48, CH), BF16),
             pltpu.VMEM((3, 4, 48, CH), BF16),
+            dma((2, 3)), dma((2, 3)), dma((2,)), dma((2,)),
+            dma((2, 3)), dma((2, 3)), dma((2,)), dma((2,)), dma((2,)), dma((2,)),
             *three, *nine, *nine, *nine, *nine, *nine, *three,
+            *swap_sems(),
         ],
-        compiler_params=params(collective_id=3, has_side_effects=True),
-        cost_estimate=pl.CostEstimate(flops=20 * 2**30, bytes_accessed=14 * 2**20, transcendentals=0),
-    )(wide1, pg, wide2, g, x, k2)
-
-
-def source_kernel(slot, got_ref, w_ref, ps_ref, sums_ref, out_ref, one_ref, two_ref, rows, wexp):
-    for i in range(3):
-        one_ref[i] = sums_ref[0, i].astype(F32)
-        two_ref[i] = sums_ref[1, i].astype(F32)
-
-    def take(p, carry):
-        rows[pl.ds(pl.multiple_of(p * BT, BT), BT), :] = got_ref[slot[p]]
-        return carry
-
-    lax.fori_loop(0, PAIRS, take, 0, unroll=4)
-    w = w_ref[...]
-    ps = ps_ref[...]
-    for s in range(SB):
-        wexp[s * BL : (s + 1) * BL, :] = w * (ps == s).astype(F32).astype(BF16)
-    for m in range(4):
-        out_ref[m * 256 : (m + 1) * 256, :] = jnp.dot(
-            wexp[m * 256 : (m + 1) * 256, :], rows[...], preferred_element_type=F32
-        ).astype(BF16)
-
-
-def source_side(slot, returned, w_cells, ps_cells, sums):
-    return pl.pallas_call(
-        source_kernel,
-        name="source_grad",
-        out_shape=(
-            jax.ShapeDtypeStruct((SB * BL, CH), BF16),
-            jax.ShapeDtypeStruct((3, PART, CH), F32),
-            jax.ShapeDtypeStruct((3, PART, CH), F32),
-        ),
-        in_specs=[SM, VM, VM, VM, VM],
-        out_specs=(VM, VM, VM),
-        scratch_shapes=[
-            pltpu.VMEM((PAIRS * BT, CH), BF16),
-            pltpu.VMEM((SB * BL, PAIRS * BT), BF16),
-        ],
-        compiler_params=params(),
-        cost_estimate=pl.CostEstimate(flops=2 * 2048 * 1024 * 256, bytes_accessed=4 * 2**20, transcendentals=0),
-    )(slot, returned, w_cells, ps_cells, sums)
+        compiler_params=pltpu.CompilerParams(vmem_limit_bytes=58 * 2**20, collective_id=2, has_side_effects=True),
+        cost_estimate=pl.CostEstimate(flops=6 * 2**30, bytes_accessed=12 * 2**20, transcendentals=2**18),
+    )(flip, ids, slot, x, hidden_grad, grad, k1, k1t, k2, w_cells, ps_cells)
+
+
+PART = 3 * CH
+
+
+def axes_of(o):
+    return o, (o + 1) % 3, (o + 2) % 3
+
+
+class Sums:
+    def __init__(self, out, acc, send1, recv1, sent2, got2, sent3, got3, got4, sems):
+        self.out, self.acc, self.send1, self.recv1 = out, acc, send1, recv1
+        self.sent2, self.got2, self.sent3, self.got3, self.got4, self.sems = sent2, got2, sent3, got3, got4, sems
+        t, b, tiles, bands = place_in_mesh()
+        self.place = spot(t, b)
+        self.core = self.place[3]
+
+    def first(self, o):
+        s, r = self.sems[0:2]
+        return remote(self.send1.at[o], self.recv1.at[o], s.at[o], r.at[o], twin())
+
+    def second(self, o, k):
+        s, r = self.sems[2:4]
+        a = axes_of(o)[0]
+        at = pl.ds(pl.multiple_of(lax.rem(self.place[a] + k, 4) * 192, 64), 192)
+        return remote(self.sent2.at[o, at], self.got2.at[o, k - 1], s.at[o, k - 1], r.at[o, k - 1], axis_peer(a, k))
+
+    def third(self, o, k):
+        s, r = self.sems[4:6]
+        a = axes_of(o)[1]
+        at = pl.ds(pl.multiple_of(lax.rem(self.place[a] + k, 4) * 48, 16), 48)
+        return remote(self.sent3.at[o, at], self.got3.at[o, k - 1], s.at[o, k - 1], r.at[o, k - 1], axis_peer(a, k))
+
+    def fourth(self, o, k):
+        s, r = self.sems[6:8]
+        a = axes_of(o)[2]
+        mine = self.got4.at[o, self.place[a]]
+        return remote(mine, mine, s.at[o, k - 1], r.at[o, k - 1], axis_peer(a, k))
+
+    def rows(self, o, wide):
+        a, c, _ = axes_of(o)
+        if wide:
+            return pl.ds(pl.multiple_of(self.place[a] * 192, 64), 192)
+        return pl.ds(pl.multiple_of(self.place[a] * 192 + self.place[c] * 48, 16), 48)
+
+    def fifth(self, o, k):
+        s, r = self.sems[8:10]
+        rows = self.out.at[self.core, o, self.rows(o, False)]
+        return remote(rows, rows, s.at[o, k - 1], r.at[o, k - 1], axis_peer(axes_of(o)[1], k))
+
+    def sixth(self, o, k):
+        s, r = self.sems[10:12]
+        rows = self.out.at[self.core, o, self.rows(o, True)]
+        return remote(rows, rows, s.at[o, k - 1], r.at[o, k - 1], axis_peer(axes_of(o)[0], k))
+
+    def seventh(self, o):
+        s, r = self.sems[12:14]
+        whole = self.out.at[self.core, o]
+        return remote(whole, whole, s.at[o], r.at[o], twin())
+
+    def start(self, o):
+        self.send1[o] = self.acc[1 - self.core, o].astype(BF16)
+        self.first(o).start()
+
+    def to_second(self):
+        for o in range(3):
+            self.first(o).wait_recv()
+            total = self.acc[self.core, o] + self.recv1[o].astype(F32)
+            self.acc[self.core, o] = total
+            self.sent2[o] = total.astype(BF16)
+            for k in (2, 1, 3):
+                self.second(o, k).start()
+
+    def to_third(self):
+        for o in range(3):
+            for k in (1, 2, 3):
+                self.second(o, k).wait_recv()
+            total = self.acc[self.core, o, self.rows(o, True), :]
+            for k in (1, 2, 3):
+                total = total + self.got2[o, k - 1].astype(F32)
+            self.acc[self.core, o, 0:192, :] = total
+            self.sent3[o] = total.astype(BF16)
+            for k in (2, 1, 3):
+                self.third(o, k).start()
+
+    def to_fourth(self):
+        for o in range(3):
+            a, c, e = axes_of(o)
+            for k in (1, 2, 3):
+                self.third(o, k).wait_recv()
+            total = self.acc[self.core, o, pl.ds(pl.multiple_of(self.place[c] * 48, 16), 48), :]
+            for k in (1, 2, 3):
+                total = total + self.got3[o, k - 1].astype(F32)
+            self.got4[o, self.place[e]] = total.astype(BF16)
+            for k in (2, 1, 3):
+                self.fourth(o, k).start()
+
+    def to_fifth(self):
+        for o in range(3):
+            for k in (1, 2, 3):
+                self.fourth(o, k).wait_recv()
+            v = [self.got4[o, q].astype(F32) for q in range(4)]
+            self.out[self.core, o, self.rows(o, False), :] = (((v[0] + v[1]) + v[2]) + v[3]).astype(BF16)
+            for k in (2, 1, 3):
+                self.fifth(o, k).start()
+
+    def to_sixth(self):
+        for o in range(3):
+            for k in (1, 2, 3):
+                self.fifth(o, k).wait_recv()
+            for k in (2, 1, 3):
+                self.sixth(o, k).start()
+
+    def to_seventh(self):
+        for o in range(3):
+            for k in (1, 2, 3):
+                self.sixth(o, k).wait_recv()
+            self.seventh(o).start()
+
+    def finish(self):
+        for o in range(3):
+            self.seventh(o).wait_recv()
+        for o in range(3):
+            self.first(o).wait_send()
+            self.seventh(o).wait_send()
+            for k in (1, 2, 3):
+                for step in (self.second, self.third, self.fourth, self.fifth, self.sixth):
+                    step(o, k).wait_send()
 
 
 def local(
@@ -787,10 +932,11 @@
     me = lax.axis_index(axes)
     target = pair_target[:, 0]
     outgoing, slot = regrid(target, pair_source, regrid_weights, source_cells)
-    arrived = lax.all_to_all(outgoing, axes, split_axis=0, concat_axis=0, tiled=True)
     upstream = out_grad[0]
     named = (target * BLOCKS + pair_block)[None, :]
-    hidden_grad, k1_back, table = back(flip_codes, named, upstream, kernel_one, kernel_two)
+    hidden_grad, k1_back, table, arrived = back(
+        flip_codes, named, upstream, kernel_one, kernel_two, outgoing.reshape(WORLD)
+    )
     table = table[:, 0, :]
     order = lax.broadcasted_iota(jnp.int32, table.shape, 1)
     mine = (table // BLOCKS) == me
@@ -800,33 +946,27 @@
     id_first = jnp.sum(jnp.where(order == first, block, 0), axis=1) + jnp.where(first[:, 0] == PAIRS, BLOCKS, 0)
     more = last > first
     id_last = jnp.sum(jnp.where((order == last) & more, block, 0), axis=1) + jnp.where(more[:, 0], 0, BLOCKS)
-    ids = jnp.stack([id_first, id_last], axis=1).reshape(2 * PAIRS)
-    regridded = gather_sum(ids, arrived)
-    back_rows, wide1, wide2, pre_grad = mid(
+    ids = jnp.concatenate([id_first, id_last])
+    regridded = gather_sum(ids, arrived.reshape(2, 2 * PAIRS, BT, 128))
+    w_cells = regrid_weights.transpose(2, 0, 1).reshape(BL, PAIRS * BT)
+    ps_cells = jnp.repeat(pair_source, BT)[None, :]
+    mixed, sums, source_grad = mid(
         flip_codes,
         jnp.minimum(ids, BLOCKS - 1),
+        slot,
         regridded.reshape(ROWS, COLS, CH),
         hidden_grad,
         upstream.reshape(CELLS, CH),
-        kernel_one.reshape(3, 3 * CH, CH),
+        kernel_one.reshape(3, PART, CH),
         k1_back,
+        kernel_two.reshape(3, PART, CH),
+        w_cells,
+        ps_cells,
     )
-    returned = lax.all_to_all(back_rows, axes, split_axis=0, concat_axis=0, tiled=True)
-    mixed, sums = kernel_sums(
-        wide1,
-        pre_grad,
-        wide2,
-        upstream.reshape(CELLS, CH),
-        regridded.reshape(CELLS, CH),
-        kernel_two.reshape(3, PART, CH),
-    )
-    w_cells = regrid_weights.transpose(2, 0, 1).reshape(BL, PAIRS * BT)
-    ps_cells = jnp.repeat(pair_source, BT)[None, :]
-    source_grad, one, two = source_side(slot, returned, w_cells, ps_cells, sums)
     return (
         mixed.reshape(1, ROWS, COLS, CH),
-        one.reshape(3, 3, CH, CH),
-        two.reshape(3, 3, CH, CH),
+        sums[0].astype(F32).reshape(3, 3, CH, CH),
+        sums[1].astype(F32).reshape(3, 3, CH, CH),
         source_grad,
     )
 

time: 163 us -> 148 us (0.908)
  starting transfers between devices: 19.1 us -> 0 us
  local copies, waits for them, and re-layouts: 19.8 us -> 12.3 us
  Pallas kernels: 122 us -> 129 us
  other arithmetic: 0.36 us -> 5.19 us
    pallas_call x2 -> x0, Pallas kernels: 54.1 us -> none  [the longest x1 49.5 us: kernel_sums(): pl.pallas_call(sum_kernel, name='kernel_sums', out_shape=(jax.ShapeDtypeS...]
    pallas_call x1, Pallas kernels: 25.3 us -> 75 us  [mid(): pl.pallas_call(mid_kernel, name='middle', out_shape=(jax.ShapeDtypeStruct...]
    all_to_all x2 -> x0, starting transfers between devices: 19.1 us -> none  [the longest x1 11.5 us: local(): lax.all_to_all(outgoing, axes, split_axis=0, concat_axis=0, tiled=True)]
    unnamed x50 -> x35, local copies, waits for them, and re-layouts: 18.8 us -> 6.79 us
    pallas_call x1, Pallas kernels: 33.7 us -> 44.9 us  [back(): pl.pallas_call(back_kernel, name='hidden_adjoint', out_shape=(jax.ShapeDt...]
    convert_element_type x0 -> x2, other arithmetic: none -> 3.26 us  [the longest x1 1.63 us: local(): sums[0].astype(F32).reshape(3, 3, CH, CH)]
    slice x0 -> x1, local copies, waits for them, and re-layouts: none -> 1.78 us  [local(): sums[1].astype(F32).reshape(3, 3, CH, CH)]
  transfers between devices with their start and end apart: 2 -> 0, of which waited for: 0 -> 0; matrix products, arithmetic and copies ran while one was open for 1% -> 0% of each run, Pallas kernels for 51% -> 0%
where the time goes in v1:
time: 148 us
  Pallas kernels  129 us (87%)
  local copies, waits for them, and re-layouts  12.3 us (8%)
  other arithmetic  5.19 us (4%)
    pallas_call x1, Pallas kernels, mid(): pl.pallas_call(mid_kernel, name='middle', out_shape=(jax.ShapeDtypeStruct...  75 us
    pallas_call x1, Pallas kernels, back(): pl.pallas_call(back_kernel, name='hidden_adjoint', out_shape=(jax.ShapeDt...  44.9 us
    pallas_call x1, Pallas kernels, regrid(): pl.pallas_call(regrid_kernel, name='regrid', out_shape=(jax.ShapeDtypeStr...  7.25 us
    unnamed x35, local copies, waits for them, and re-layouts  6.79 us

profile of v1, /device:TPU:1, one launch (start us, length us, event | category | flops | bytes accessed | tf_op | source)
XLA Modules:
  0.0 147.6 jit_solution(6551341370788527597)
XLA Ops:
  0.6 0.0 copy-start.13
  0.6 0.7 add_bitcast_fusion.own_ref
  1.4 0.7 broadcast_in_dim.26
  2.1 0.7 broadcast_in_dim_reshape.3.ps_ref
  2.8 0.0 copy-start.2
  2.8 0.0 copy-start.5
  2.8 0.0 copy-start.7
  2.8 1.4 copy.16
  4.2 0.9 copy.17.w_ref
  5.1 0.0 copy-done.13
  5.1 0.4 copy.15.w_ref
  5.6 0.0 copy-done.2
  5.6 0.0 copy-done.5
  5.6 0.0 copy-done.7
  5.6 0.0 copy-start.3
  5.6 0.0 copy-start.4
  5.6 0.0 copy-start.6
  5.7 0.0 copy-start.8
  5.7 7.2 %regrid.1 = (bf16[2,256,16,128]{3,2,1,0:T(8,128)(2,1)S(1)}, s32[128]{0:T(128)S(1)}) custom-call(s32[128]{0:T(128)S(1)} %bitcast.27, s32[128]{0:T(128)S(1)} %copy-done.2, bf16[128,16,64]{2,1,0:T(8,128)(2,1)S(1)} %copy.15.w_ref, bf16[1024,256]{1,0:T(8,128)(2,1)S(1)} %copy-done.5), custom_call_target="tpu_custom_call" | custom-call | flops 1073741824 | bytes 6291456 | tf_op jit(solution)/shard_map/regrid/pallas_call | solution.py:64
  12.9 0.0 copy-start.9
  12.9 1.3 copy-done.9
  14.2 0.0 copy-start.12
  14.2 0.6 copy-done.12
  14.8 0.0 copy-done.3
  14.8 0.0 copy-done.4
  14.8 0.0 copy-done.6
  14.8 0.0 copy-done.8
  14.8 44.9 %hidden_adjoint.1 = (f32[1024,256]{1,0:T(8,128)S(1)}, bf16[3,768,256]{2,1,0:T(8,128)(2,1)S(1)}, s32[128,1,128]{2,1,0:T(1,128)S(1)}, bf16[4,4,2,4,2,2,16,128]{7,6,5,4,3,2,1,0:T(8,128)(2,1)}) custom-call(s32[32]{0:T(128)S(1)} %copy-done.8, s32[1,128]{1,0:T(1,128)S(1)} %add_bitcast_fusion.own_ref, bf16[8,128,256]{2,1,0:T(8,128)(2,1)S(1)} %bitcast.26, ...), custom_call_target="tpu_custom_call" | custom-call | flops 6442450944 | bytes 8388608 | tf_op jit(solution)/shard_map/hidden_adjoint/pallas_call | solution.py:569
  59.7 0.0 copy-start.10
  59.7 0.0 copy-start.11
  59.7 0.1 select_reduce_fusion.3
  59.9 0.2 select_reduce_fusion.2
  60.1 0.9 pad_add_fusion
  61.0 0.0 copy-start
  61.0 1.6 %copy-done = bf16[4,4,2,4,2,2,16,128]{7,6,5,4,3,2,1,0:T(8,128)(2,1)S(1)} copy-done((bf16[4,4,2,4,2,2,16,128]{7,6,5,4,3,2,1,0:T(8,128)(2,1)S(1)}, bf16[4,4,2,4,2,2,16,128]{7,6,5,4,3,2,1,0:T(8,128)(2,1)}, u32[]{:S(2)}) %copy-start) | copy-done | bytes 2097176
  62.6 2.1 %gather_sum.1 = bf16[64,16,256]{2,1,0:T(8,128)(2,1)S(1)} custom-call(s32[256]{0:T(256)S(1)} %get-tuple-element.28.ids, bf16[2,256,16,128]{3,2,1,0:T(8,128)(2,1)S(1)} %bitcast.19), custom_call_target="tpu_custom_call" | custom-call | flops 2097152 | bytes 3145728 | tf_op jit(solution)/shard_map/gather_sum/pallas_call | solution.py:97
  64.6 0.0 copy-done.10
  64.7 0.0 copy-done.11
  64.7 0.0 copy-start.1
  64.7 0.8 copy-done.1
  65.5 75.0 %middle.1 = (bf16[1024,256]{1,0:T(8,128)(2,1)}, bf16[2,3,768,256]{3,2,1,0:T(8,128)(2,1)}, bf16[1024,256]{1,0:T(8,128)(2,1)}) custom-call(s32[32]{0:T(128)} %flip.3, s32[256]{0:T(256)} %get-tuple-element.29.ids, s32[128]{0:T(128)} %copy-done.12, bf16[8,128,256]{2,1,0:T(8,128)(2,1)} %bitcast.20, f32[1024,256]{1,0:T(8,128)} %copy-done.11, ...), custom_call_target="tpu_custom_call" | custom-call | flops 6442450944 | bytes 12582912 | tf_op jit(solution)/shard_map/middle/pallas_call | solution.py:751
  140.5 1.8 %fusion.5 = (bf16[1,3,768,256]{3,2,1,0:T(8,128)(2,1)S(1)}, bf16[1,3,768,256]{3,2,1,0:T(8,128)(2,1)S(1)}) fusion(bf16[2,3,768,256]{3,2,1,0:T(8,128)(2,1)} %get-tuple-element.20), kind=kLoop, calls=%fused_computation.22 | loop fusion | bytes 4718592 | tf_op jit(solution)/shard_map/slice | solution.py:969
  142.3 1.6 %convert.2 = f32[3,3,256,256]{3,2,1,0:T(8,128)} convert(bf16[3,3,256,256]{3,2,1,0:T(8,128)(2,1)S(1)} %bitcast.30) | non-fusion elementwise | flops 589824 | bytes 3538944 | tf_op jit(solution)/shard_map/convert_element_type | solution.py:968
  143.9 1.6 %convert.3 = f32[3,3,256,256]{3,2,1,0:T(8,128)} convert(bf16[3,3,256,256]{3,2,1,0:T(8,128)(2,1)S(1)} %bitcast.29) | non-fusion elementwise | flops 589824 | bytes 3538944 | tf_op jit(solution)/shard_map/convert_element_type | solution.py:969
  145.6 0.0 copy-done.15
  145.6 0.8 copy.20
  146.4 0.4 copy-done.14
  146.8 0.8 copy.21
  (4 shorter events, 0.0 us)
Async XLA Ops:
  0.6 4.5 %copy-start.13 = (bf16[128,16,64]{0,2,1:T(8,128)(2,1)S(1)}, bf16[128,16,64]{0,2,1:T(8,128)(2,1)}, u32[]{:S(2)}) copy-start(bf16[128,16,64]{0,2,1:T(8,128)(2,1)} %param.10) | copy-start | bytes 786436
  2.8 2.8 %copy-start.2 = (s32[128]{0:T(128)S(1)}, s32[128]{0:T(128)}, u32[]{:S(2)}) copy-start(s32[128]{0:T(128)} %psrc.1) | copy-start | bytes 1540
  2.8 2.8 %copy-start.5 = (bf16[1024,256]{1,0:T(8,128)(2,1)S(1)}, bf16[1024,256]{1,0:T(8,128)(2,1)}, u32[]{:S(2)}) copy-start(bf16[1024,256]{1,0:T(8,128)(2,1)} %src_ref.1) | copy-start | bytes 1572868
  2.8 2.8 %copy-start.7 = (s32[128,1]{0,1:T(1,128)S(1)}, s32[128,1]{0,1:T(1,128)}, u32[]{:S(2)}) copy-start(s32[128,1]{0,1:T(1,128)} %param.11) | copy-start | bytes 1540
  5.6 9.2 %copy-start.3 = (bf16[3,3,256,256]{3,2,1,0:T(8,128)(2,1)S(1)}, bf16[3,3,256,256]{3,2,1,0:T(8,128)(2,1)}, u32[]{:S(2)}) copy-start(bf16[3,3,256,256]{3,2,1,0:T(8,128)(2,1)} %k1_ref.1) | copy-start | bytes 3538948
  5.6 9.2 %copy-start.4 = (bf16[3,3,256,256]{3,2,1,0:T(8,128)(2,1)S(1)}, bf16[3,3,256,256]{3,2,1,0:T(8,128)(2,1)}, u32[]{:S(2)}) copy-start(bf16[3,3,256,256]{3,2,1,0:T(8,128)(2,1)} %k2_ref.1) | copy-start | bytes 3538948
  5.6 9.2 %copy-start.6 = (bf16[1,8,128,256]{3,2,1,0:T(8,128)(2,1)S(1)}, bf16[1,8,128,256]{3,2,1,0:T(8,128)(2,1)}, u32[]{:S(2)}) copy-start(bf16[1,8,128,256]{3,2,1,0:T(8,128)(2,1)} %param.17) | copy-start | bytes 1572868
  5.7 9.2 %copy-start.8 = (s32[32]{0:T(128)S(1)}, s32[32]{0:T(128)}, u32[]{:S(2)}) copy-start(s32[32]{0:T(128)} %flip.3) | copy-start | bytes 388
  12.9 1.3 copy-start.9
  14.2 0.6 copy-start.12
  59.7 4.9 %copy-start.10 = (bf16[3,768,256]{2,1,0:T(8,128)(2,1)}, bf16[3,768,256]{2,1,0:T(8,128)(2,1)S(1)}, u32[]{:S(2)}) copy-start(bf16[3,768,256]{2,1,0:T(8,128)(2,1)S(1)} %get-tuple-element.18.k1t_ref) | copy-start | bytes 3538948
  59.7 4.9 %copy-start.11 = (f32[1024,256]{1,0:T(8,128)}, f32[1024,256]{1,0:T(8,128)S(1)}, u32[]{:S(2)}) copy-start(f32[1024,256]{1,0:T(8,128)S(1)} %get-tuple-element.17.hg_ref) | copy-start | bytes 3145732
  61.0 1.6 %copy-start = (bf16[4,4,2,4,2,2,16,128]{7,6,5,4,3,2,1,0:T(8,128)(2,1)S(1)}, bf16[4,4,2,4,2,2,16,128]{7,6,5,4,3,2,1,0:T(8,128)(2,1)}, u32[]{:S(2)}) copy-start(bf16[4,4,2,4,2,2,16,128]{7,6,5,4,3,2,1,0:T(8,128)(2,1)} %get-tuple-element.16) | copy-start | bytes 6291460
  64.7 0.8 copy-start.1
  143.9 1.6 %copy-start.15 = (bf16[1024,256]{1,0:T(8,128)(2,1)S(1)}, bf16[1024,256]{1,0:T(8,128)(2,1)}, u32[]{:S(2)}) copy-start(bf16[1024,256]{1,0:T(8,128)(2,1)} %get-tuple-element.19) | copy-start | bytes 1572868
  145.6 1.2 copy-start.14

commit v2 on v1

--- a/solution.py
+++ b/solution.py
@@ -10,7 +10,7 @@
 MESH = pl.DeviceIdType.MESH
 VM = pl.BlockSpec(memory_space=pltpu.VMEM)
 SM = pl.BlockSpec(memory_space=pltpu.SMEM)
-LIMIT = 48 * 2**20
+LIMIT = 16 * 2**20
 ROWS, COLS, CH = 8, 128, 256
 PAIRS, BT, BL, SB, BLOCKS = 128, 16, 64, 16, 64
 CELLS = ROWS * COLS
@@ -84,7 +84,7 @@
     acc[...] = jnp.zeros_like(acc)
 
     def add(q, c):
-        k = ids[q]
+        k = ids[lax.div(q, PAIRS), lax.rem(q, PAIRS)]
         for h in (0, 1):
             acc[k, :, h * 128 : (h + 1) * 128] += got_ref[h, q].astype(F32)
         return c
@@ -511,13 +511,14 @@
 
 
 def back_kernel(
-    flip, own_ref, g_ref, k1_ref, k2_ref, outgoing, hg_ref, k1t_ref, tab, arrived,
-    ext, send, recv, tmp, rim, trim, wide, k2t, b1, b2, b3, ss, rs, rss, rrs, tss, trs, *sems,
+    flip, tgt_ref, blk_ref, src_row, w_ref, g_ref, k1_ref, k2_ref, outgoing,
+    hg_ref, k1t_ref, arrived, ids_ref, safe_ref, w_cells, ps_cells,
+    tab, ext, send, recv, tmp, rim, trim, wide, k2t, b1, b2, b3, ss, rs, rss, rrs, tss, trs, *sems,
 ):
     d = 2
     swap = Swap((outgoing, b1, b2, b3, arrived), sems)
     t, b, tiles, bands = place_in_mesh()
-    tab[t * 4 + b] = own_ref[...]
+    tab[t * 4 + b] = tgt_ref[...] * BLOCKS + blk_ref[...]
     me, before, after = flags(flip)
     ext[pl.ds(d, ROWS)] = g_ref[...]
     make_slab(ext, d, send, 0, me, tmp)
@@ -526,27 +527,24 @@
     greet_table()
     greet_axes()
     greet(sum(TABLE_PEERS) + AXIS_PEERS)
-    for hs in range(4):
-        swap.core_start(hs)
     table_start(tab, tss, trs, 0)
     start_sides(send, recv, ss, rs)
     start_rows(ext, d, rss, rrs)
+    for hs in range(4):
+        swap.core_start(hs)
+    for i in range(3):
+        for j in range(3):
+            k2t[i, j * CH : (j + 1) * CH, :] = k2_ref[2 - i, 2 - j].T
     table_wait(tab, tss, trs, 0)
     table_start(tab, tss, trs, 1)
     swap.first_stage()
-    for i in range(3):
-        for j in range(3):
-            k2t[i, j * CH : (j + 1) * CH, :] = k2_ref[2 - i, 2 - j].T
-            k1t_ref[i, j * CH : (j + 1) * CH, :] = k1_ref[2 - i, 2 - j].T
-    table_wait(tab, tss, trs, 1)
-    table_start(tab, tss, trs, 2)
     wait_sides_recv(send, recv, ss, rs)
     wait_rows_recv(ext, d, rss, rrs)
     open_slab(recv, d, 0, me, rim)
     split_rim(rim, d, me, before, after, trim)
     widen(ext, d, rim, wide)
-    table_wait(tab, tss, trs, 2)
-    table_start(tab, tss, trs, 3)
+    table_wait(tab, tss, trs, 1)
+    table_start(tab, tss, trs, 2)
     swap.next_stage(1)
 
     def block(n, carry):
@@ -556,15 +554,42 @@
 
     lax.fori_loop(0, CELLS // STEP, block, 0)
     turned_part(trim, d, k2t, hg_ref)
+    table_wait(tab, tss, trs, 2)
+    table_start(tab, tss, trs, 3)
     swap.next_stage(2)
+    for i in range(3):
+        for j in range(3):
+            k1t_ref[i, j * CH : (j + 1) * CH, :] = k1_ref[2 - i, 2 - j].T
+    for n in range(SB):
+        part = w_ref[n * 8 : (n + 1) * 8].reshape(128, BL).astype(F32)
+        part = jnp.concatenate([part, part], axis=1).T
+        w_cells[:, n * 128 : (n + 1) * 128] = part[0:BL].astype(BF16)
+    spread = (
+        lax.broadcasted_iota(jnp.int32, (PAIRS, PAIRS * BT), 1) // BT
+        == lax.broadcasted_iota(jnp.int32, (PAIRS, PAIRS * BT), 0)
+    ).astype(F32)
+    own = jnp.broadcast_to(src_row[...], (8, PAIRS)).astype(F32)
+    ps_cells[...] = jnp.dot(own.astype(BF16), spread.astype(BF16), preferred_element_type=F32)
     table_wait(tab, tss, trs, 3)
+    table = tab[...].reshape(PAIRS, PAIRS).T
+    order = lax.broadcasted_iota(jnp.int32, (PAIRS, PAIRS), 0)
+    block_of = lax.bitwise_and(table, BLOCKS - 1)
+    mine = lax.shift_right_logical(table, 6) == t * 4 + b
+    first = jnp.min(jnp.where(mine, order, PAIRS), axis=0, keepdims=True)
+    last = jnp.max(jnp.where(mine, order, -1), axis=0, keepdims=True)
+    id_first = jnp.sum(jnp.where(order == first, block_of, 0), axis=0, keepdims=True)
+    id_last = jnp.sum(jnp.where(order == last, block_of, 0), axis=0, keepdims=True)
+    ids_ref[0:1, :] = jnp.where(first < PAIRS, id_first, BLOCKS)
+    ids_ref[1:2, :] = jnp.where(last > first, id_last, BLOCKS)
+    safe_ref[0:1, :] = id_first
+    safe_ref[1:2, :] = id_last
     wait_sides_send(send, recv, ss, rs)
     wait_rows_send(ext, d, rss, rrs)
     swap.last_wait()
     swap.drain()
 
 
-def back(flip, own, grad, k1, k2, outgoing):
+def back(flip, target, block, source, weights, grad, k1, k2, outgoing):
     d = 2
     return pl.pallas_call(
         back_kernel,
@@ -572,12 +597,16 @@
         out_shape=(
             jax.ShapeDtypeStruct((CELLS, CH), F32),
             jax.ShapeDtypeStruct((3, 3 * CH, CH), BF16),
-            jax.ShapeDtypeStruct((PAIRS, 1, PAIRS), jnp.int32),
             jax.ShapeDtypeStruct(WORLD, BF16),
+            jax.ShapeDtypeStruct((2, PAIRS), jnp.int32),
+            jax.ShapeDtypeStruct((2, PAIRS), jnp.int32),
+            jax.ShapeDtypeStruct((BL, PAIRS * BT), BF16),
+            jax.ShapeDtypeStruct((8, PAIRS * BT), F32),
         ),
-        in_specs=[SM, VM, VM, VM, VM, VM],
-        out_specs=(VM, VM, VM, VM),
+        in_specs=[SM] + [VM] * 8,
+        out_specs=(VM,) * 7,
         scratch_shapes=[
+            pltpu.VMEM((PAIRS, 1, PAIRS), jnp.int32),
             pltpu.VMEM((ROWS + 2 * d, COLS, CH), BF16),
             pltpu.VMEM((2, 16, CH), BF16),
             pltpu.VMEM((2, 3, 16, CH), BF16),
@@ -597,9 +626,9 @@
             pltpu.SemaphoreType.DMA((4, 3)),
             *swap_sems(),
         ],
-        compiler_params=params(collective_id=1, has_side_effects=True),
+        compiler_params=pltpu.CompilerParams(vmem_limit_bytes=18 * 2**20, collective_id=1, has_side_effects=True),
         cost_estimate=pl.CostEstimate(flops=6 * 2**30, bytes_accessed=8 * 2**20, transcendentals=0),
-    )(flip, own, grad, k1, k2, outgoing)
+    )(flip, target, block, source, weights, grad, k1, k2, outgoing)
 
 
 def mid_kernel(
@@ -669,7 +698,7 @@
     for half in (0, 1):
 
         def pick(q, carry):
-            block = rounded[ids[half * PAIRS + q]]
+            block = rounded[ids[half, q]]
             y, zh, x = lax.div(q, 32), lax.rem(lax.div(q, 16), 2), lax.rem(lax.div(q, 4), 4)
             zl, c = lax.rem(lax.div(q, 2), 2), lax.rem(q, 2)
             b0[half, y, zh, x, zl, c] = block[:, 0:128]
@@ -710,7 +739,7 @@
 
     lax.fori_loop(0, CELLS // STEP, block, 0)
     w = w_ref[...]
-    ps = ps_ref[...]
+    ps = ps_ref[0:1, :]
     for n in range(SB):
         wexp[n * BL : (n + 1) * BL, :] = w * (ps == n).astype(F32).astype(BF16)
     sums.to_third()
@@ -792,7 +821,7 @@
             *three, *nine, *nine, *nine, *nine, *nine, *three,
             *swap_sems(),
         ],
-        compiler_params=pltpu.CompilerParams(vmem_limit_bytes=58 * 2**20, collective_id=2, has_side_effects=True),
+        compiler_params=pltpu.CompilerParams(vmem_limit_bytes=42 * 2**20, collective_id=2, has_side_effects=True),
         cost_estimate=pl.CostEstimate(flops=6 * 2**30, bytes_accessed=12 * 2**20, transcendentals=2**18),
     )(flip, ids, slot, x, hidden_grad, grad, k1, k1t, k2, w_cells, ps_cells)
 
@@ -925,34 +954,63 @@
                     step(o, k).wait_send()
 
 
+def finish_kernel(sums, mixed, source, one, two, mixed_out, source_out, wide, sems):
+    copies = [
+        pltpu.make_async_copy(mixed, mixed_out, sems.at[6]),
+        pltpu.make_async_copy(source, source_out, sems.at[7]),
+    ]
+    for copy in copies:
+        copy.start()
+    for n, out in ((0, one), (1, two)):
+        for i in range(3):
+            wide[n, i] = sums[n, i].astype(F32)
+            copy = pltpu.make_async_copy(wide.at[n, i], out.at[i], sems.at[n * 3 + i])
+            copy.start()
+            copies.append(copy)
+    for copy in copies:
+        copy.wait()
+
+
+def finish(sums, mixed, source):
+    away = pl.BlockSpec(memory_space=pltpu.HBM)
+    return pl.pallas_call(
+        finish_kernel,
+        name="finish",
+        out_shape=(
+            jax.ShapeDtypeStruct((3, PART, CH), F32),
+            jax.ShapeDtypeStruct((3, PART, CH), F32),
+            jax.ShapeDtypeStruct((CELLS, CH), BF16),
+            jax.ShapeDtypeStruct((SB * BL, CH), BF16),
+        ),
+        in_specs=[VM] * 3,
+        out_specs=(away,) * 4,
+        scratch_shapes=[pltpu.VMEM((2, 3, PART, CH), F32), pltpu.SemaphoreType.DMA((8,))],
+        compiler_params=params(),
+        cost_estimate=pl.CostEstimate(flops=2**20, bytes_accessed=8 * 2**20, transcendentals=0),
+    )(sums, mixed, source)
+
+
 def local(
     source_cells, regrid_weights, pair_target, pair_block, pair_source, flip_codes, kernel_one, kernel_two, out_grad
 ):
-    axes = ("tile", "band")
-    me = lax.axis_index(axes)
     target = pair_target[:, 0]
     outgoing, slot = regrid(target, pair_source, regrid_weights, source_cells)
     upstream = out_grad[0]
-    named = (target * BLOCKS + pair_block)[None, :]
-    hidden_grad, k1_back, table, arrived = back(
-        flip_codes, named, upstream, kernel_one, kernel_two, outgoing.reshape(WORLD)
+    hidden_grad, k1_back, arrived, ids, safe_ids, w_cells, ps_cells = back(
+        flip_codes,
+        pair_target.reshape(1, PAIRS),
+        pair_block.reshape(1, PAIRS),
+        pair_source.reshape(1, PAIRS),
+        regrid_weights,
+        upstream,
+        kernel_one,
+        kernel_two,
+        outgoing.reshape(WORLD),
     )
-    table = table[:, 0, :]
-    order = lax.broadcasted_iota(jnp.int32, table.shape, 1)
-    mine = (table // BLOCKS) == me
-    first = jnp.min(jnp.where(mine, order, PAIRS), axis=1, keepdims=True)
-    last = jnp.max(jnp.where(mine, order, -1), axis=1, keepdims=True)
-    block = table % BLOCKS
-    id_first = jnp.sum(jnp.where(order == first, block, 0), axis=1) + jnp.where(first[:, 0] == PAIRS, BLOCKS, 0)
-    more = last > first
-    id_last = jnp.sum(jnp.where((order == last) & more, block, 0), axis=1) + jnp.where(more[:, 0], 0, BLOCKS)
-    ids = jnp.concatenate([id_first, id_last])
     regridded = gather_sum(ids, arrived.reshape(2, 2 * PAIRS, BT, 128))
-    w_cells = regrid_weights.transpose(2, 0, 1).reshape(BL, PAIRS * BT)
-    ps_cells = jnp.repeat(pair_source, BT)[None, :]
     mixed, sums, source_grad = mid(
         flip_codes,
-        jnp.minimum(ids, BLOCKS - 1),
+        safe_ids,
         slot,
         regridded.reshape(ROWS, COLS, CH),
         hidden_grad,
@@ -963,10 +1021,11 @@
         w_cells,
         ps_cells,
     )
+    one, two, mixed, source_grad = finish(sums, mixed, source_grad)
     return (
         mixed.reshape(1, ROWS, COLS, CH),
-        sums[0].astype(F32).reshape(3, 3, CH, CH),
-        sums[1].astype(F32).reshape(3, 3, CH, CH),
+        one.reshape(3, 3, CH, CH),
+        two.reshape(3, 3, CH, CH),
         source_grad,
     )
 

time: 148 us -> 128 us (0.86)
  local copies, waits for them, and re-layouts: 12.3 us -> 3.75 us
  Pallas kernels: 129 us -> 123 us
  other arithmetic: 5.19 us -> 0 us
    pallas_call x1, Pallas kernels: 44.9 us -> 39.9 us  [back(): pl.pallas_call(back_kernel, name='hidden_adjoint', out_shape=(jax.ShapeDt...]
    pallas_call x1, Pallas kernels: 75 us -> 71.4 us  [mid(): pl.pallas_call(mid_kernel, name='middle', out_shape=(jax.ShapeDtypeStruct...]
    convert_element_type x2 -> x0, other arithmetic: 3.26 us -> none  [the longest x1 1.63 us: local(): sums[0].astype(F32).reshape(3, 3, CH, CH)]
    unnamed x35 -> x21, local copies, waits for them, and re-layouts: 6.79 us -> 3.75 us
    pallas_call x0 -> x1, Pallas kernels: none -> 2.57 us  [finish(): pl.pallas_call(finish_kernel, name='finish', out_shape=(jax.ShapeDtypeStr...]
    slice x1 -> x0, local copies, waits for them, and re-layouts: 1.78 us -> none  [local(): sums[1].astype(F32).reshape(3, 3, CH, CH)]
where the time goes in v2:
time: 128 us
  Pallas kernels  123 us (96%)
  local copies, waits for them, and re-layouts  3.75 us (3%)
    pallas_call x1, Pallas kernels, mid(): pl.pallas_call(mid_kernel, name='middle', out_shape=(jax.ShapeDtypeStruct...  71.4 us
    pallas_call x1, Pallas kernels, back(): pl.pallas_call(back_kernel, name='hidden_adjoint', out_shape=(jax.ShapeDt...  39.9 us
    pallas_call x1, Pallas kernels, regrid(): pl.pallas_call(regrid_kernel, name='regrid', out_shape=(jax.ShapeDtypeStr...  7.26 us
    unnamed x21, local copies, waits for them, and re-layouts  3.75 us
    pallas_call x1, Pallas kernels, finish(): pl.pallas_call(finish_kernel, name='finish', out_shape=(jax.ShapeDtypeStr...  2.57 us

profile of v2, /device:TPU:1, one launch (start us, length us, event | category | flops | bytes accessed | tf_op | source)
XLA Modules:
  0.0 128.1 jit_solution(7554643782234355578)
XLA Ops:
  0.6 1.4 %copy.14.w_ref = bf16[128,16,64]{2,1,0:T(8,128)(2,1)S(1)} copy(bf16[128,16,64]{0,2,1:T(8,128)(2,1)} %param.10) | data formatting | bytes 524288 | tf_op args[1]
  2.0 0.0 copy-start.2
  2.0 1.0 copy-done.2
  3.1 0.0 copy-start.4
  3.1 0.7 copy-done.4
  3.7 0.0 copy-start.7
  3.7 0.7 copy-done.7
  4.4 0.0 copy-start
  4.4 0.0 copy-start.1
  4.4 0.0 copy-start.3
  4.4 0.0 copy-start.5
  4.4 0.0 copy-start.6
  4.4 0.0 copy-start.8
  4.4 0.0 copy-start.9
  4.4 7.3 %regrid.1 = (bf16[2,256,16,128]{3,2,1,0:T(8,128)(2,1)S(1)}, s32[128]{0:T(128)S(1)}) custom-call(s32[128]{0:T(128)S(1)} %bitcast.20, s32[128]{0:T(128)S(1)} %copy-done.7, bf16[128,16,64]{2,1,0:T(8,128)(2,1)S(1)} %copy.14.w_ref, bf16[1024,256]{1,0:T(8,128)(2,1)S(1)} %copy-done.2), custom_call_target="tpu_custom_call" | custom-call | flops 1073741824 | bytes 6291456 | tf_op jit(solution)/shard_map/regrid/pallas_call | solution.py:64
  11.7 0.0 copy-done
  11.7 0.0 copy-done.1
  11.7 0.0 copy-done.3
  11.7 0.0 copy-done.5
  11.7 0.0 copy-done.6
  11.7 0.0 copy-done.8
  11.7 0.0 copy-done.9
  11.7 39.9 %hidden_adjoint.1 = (f32[1024,256]{1,0:T(8,128)S(1)}, bf16[3,768,256]{2,1,0:T(8,128)(2,1)S(1)}, bf16[4,4,2,4,2,2,16,128]{7,6,5,4,3,2,1,0:T(8,128)(2,1)S(1)}, s32...) custom-call(s32[32]{0:T(128)S(1)} %copy-done.9, ...), custom_call_target="tpu_custom_call" | custom-call | flops 6442450944 | bytes 8388608 | tf_op jit(solution)/shard_map/hidden_adjoint/pallas_call | solution.py:594
  51.7 2.2 %gather_sum.1 = bf16[64,16,256]{2,1,0:T(8,128)(2,1)S(1)} custom-call(s32[2,128]{1,0:T(2,128)S(1)} %get-tuple-element.23.ids, bf16[2,256,16,128]{3,2,1,0:T(8,128)(2,1)S(1)} %bitcast.14), custom_call_target="tpu_custom_call" | custom-call | flops 2097152 | bytes 3145728 | tf_op jit(solution)/shard_map/gather_sum/pallas_call | solution.py:97
  53.9 71.4 %middle.1 = (bf16[1024,256]{1,0:T(8,128)(2,1)S(1)}, bf16[2,3,768,256]{3,2,1,0:T(8,128)(2,1)S(1)}, bf16[1024,256]{1,0:T(8,128)(2,1)S(1)}) custom-call(s32[32]{0:T(128)S(1)} %copy-done.9, s32[2,128]{1,0:T(2,128)S(1)} %get-tuple-element.21.ids, s32[128]{0:T(128)S(1)} %get-tuple-element.22.slot, bf16[8,128,256]{2,1,0:T(8,128)(2,1)S(1)} %bitcast.15, ...), custom_call_target="tpu_custom_call" | custom-call | flops 6442450944 | bytes 12582912 | tf_op jit(solution)/shard_map/middle/pallas_call | solution.py:780
  125.3 2.6 %finish.1 = (f32[3,768,256]{2,1,0:T(8,128)}, f32[3,768,256]{2,1,0:T(8,128)}, bf16[1024,256]{1,0:T(8,128)(2,1)}, bf16[1024,256]{1,0:T(8,128)(2,1)}) custom-call(bf16[2,3,768,256]{3,2,1,0:T(8,128)(2,1)S(1)} %get-tuple-element.29.sums, bf16[1024,256]{1,0:T(8,128)(2,1)S(1)} %get-tuple-element.30.mixed, bf16[1024,256]{1,0:T(8,128)(2,1)S(1)} %get-tuple-element.31.source), custom_call_target="tpu_custom_call" | custom-call | flops 1048576 | bytes 8388608 | tf_op jit(solution)/shard_map/finish/pallas_call | solution.py:976
Async XLA Ops:
  2.0 1.0 copy-start.2
  3.1 0.7 copy-start.4
  3.7 0.7 copy-start.7
  4.4 7.3 %copy-start = (bf16[3,3,256,256]{3,2,1,0:T(8,128)(2,1)S(1)}, bf16[3,3,256,256]{3,2,1,0:T(8,128)(2,1)}, u32[]{:S(2)}) copy-start(bf16[3,3,256,256]{3,2,1,0:T(8,128)(2,1)} %k1_ref.1) | copy-start | bytes 3538948
  4.4 7.3 %copy-start.1 = (bf16[3,3,256,256]{3,2,1,0:T(8,128)(2,1)S(1)}, bf16[3,3,256,256]{3,2,1,0:T(8,128)(2,1)}, u32[]{:S(2)}) copy-start(bf16[3,3,256,256]{3,2,1,0:T(8,128)(2,1)} %k2_ref.1) | copy-start | bytes 3538948
  4.4 7.3 %copy-start.3 = (bf16[1,8,128,256]{3,2,1,0:T(8,128)(2,1)S(1)}, bf16[1,8,128,256]{3,2,1,0:T(8,128)(2,1)}, u32[]{:S(2)}) copy-start(bf16[1,8,128,256]{3,2,1,0:T(8,128)(2,1)} %param.17) | copy-start | bytes 1572868
  4.4 7.3 %copy-start.5 = (s32[128,1]{0,1:T(1,128)S(1)}, s32[128,1]{0,1:T(1,128)}, u32[]{:S(2)}) copy-start(s32[128,1]{0,1:T(1,128)} %param.11) | copy-start | bytes 1540
  4.4 7.3 %copy-start.6 = (s32[128]{0:T(128)S(1)}, s32[128]{0:T(128)}, u32[]{:S(2)}) copy-start(s32[128]{0:T(128)} %param.12) | copy-start | bytes 1540
  4.4 7.3 %copy-start.8 = (s32[128]{0:T(128)S(1)}, s32[128]{0:T(128)}, u32[]{:S(2)}) copy-start(s32[128]{0:T(128)} %psrc.1) | copy-start | bytes 1540
  4.4 7.3 %copy-start.9 = (s32[32]{0:T(128)S(1)}, s32[32]{0:T(128)}, u32[]{:S(2)}) copy-start(s32[32]{0:T(128)} %flip.3) | copy-start | bytes 388

commit v3 on v2

--- a/solution.py
+++ b/solution.py
@@ -10,6 +10,7 @@
 MESH = pl.DeviceIdType.MESH
 VM = pl.BlockSpec(memory_space=pltpu.VMEM)
 SM = pl.BlockSpec(memory_space=pltpu.SMEM)
+FAR = pl.BlockSpec(memory_space=pltpu.HBM)
 LIMIT = 16 * 2**20
 ROWS, COLS, CH = 8, 128, 256
 PAIRS, BT, BL, SB, BLOCKS = 128, 16, 64, 16, 64
@@ -20,7 +21,14 @@
     return pltpu.CompilerParams(vmem_limit_bytes=LIMIT, **more)
 
 
-def regrid_kernel(tgt, psrc, w_ref, src_ref, out_ref, slot_ref, cnt, masks, wexp):
+def regrid_kernel(tgt_far, psrc_far, w_ref, src_far, out_ref, slot_ref, cnt, masks, wexp, tgt, psrc, src_ref, sems):
+    copies = [
+        pltpu.make_async_copy(tgt_far, tgt, sems.at[0]),
+        pltpu.make_async_copy(psrc_far, psrc, sems.at[1]),
+        pltpu.make_async_copy(src_far, src_ref, sems.at[2]),
+    ]
+    for copy in copies:
+        copy.start()
     lane = lax.broadcasted_iota(jnp.int32, (BT, 128), 1)
     masks[0] = (lane < BL).astype(F32).astype(BF16)
     masks[1] = (lane >= BL).astype(F32).astype(BF16)
@@ -30,18 +38,15 @@
         cnt[i] = 0
         return c
 
-    lax.fori_loop(0, PAIRS, clear, 0)
-
-    def rank(p, c):
+    lax.fori_loop(0, PAIRS, clear, 0, unroll=8)
+    copies[0].wait()
+    copies[1].wait()
+
+    def place(p, c):
         t = tgt[p]
         r = cnt[t]
         cnt[t] = r + 1
         slot_ref[p] = jnp.minimum(r, 1) * PAIRS + t
-        return c
-
-    lax.fori_loop(0, PAIRS, rank, 0)
-
-    def place(p, c):
         s = psrc[p]
         w = w_ref[p]
         ww = jnp.concatenate([w, w], axis=1) * masks[lax.rem(s, 2)]
@@ -50,8 +55,8 @@
         wexp[pl.ds(row, BT), pl.ds(col, 128)] = ww
         return c
 
-    lax.fori_loop(0, PAIRS, place, 0, unroll=4)
-    out_ref[...] = jnp.zeros_like(out_ref)
+    lax.fori_loop(0, PAIRS, place, 0, unroll=8)
+    copies[2].wait()
     for m in range(4):
         part = jnp.dot(wexp[m * 512 : (m + 1) * 512, :], src_ref[...], preferred_element_type=F32).astype(BF16)
         for q in range(32):
@@ -68,29 +73,36 @@
             jax.ShapeDtypeStruct((2, 2 * PAIRS, BT, 128), BF16),
             jax.ShapeDtypeStruct((PAIRS,), jnp.int32),
         ),
-        in_specs=[SM, SM, VM, VM],
+        in_specs=[FAR, FAR, VM, FAR],
         out_specs=(VM, SM),
         scratch_shapes=[
             pltpu.SMEM((PAIRS,), jnp.int32),
             pltpu.VMEM((2, BT, 128), BF16),
             pltpu.VMEM((PAIRS * BT, SB * BL), BF16),
+            pltpu.SMEM((PAIRS,), jnp.int32),
+            pltpu.SMEM((PAIRS,), jnp.int32),
+            pltpu.VMEM((SB * BL, CH), BF16),
+            pltpu.SemaphoreType.DMA((3,)),
         ],
         compiler_params=params(),
         cost_estimate=pl.CostEstimate(flops=2 * 2048 * 1024 * 256, bytes_accessed=6 * 2**20, transcendentals=0),
     )(tgt, psrc, weights, source)
 
 
-def gather_sum_kernel(ids, got_ref, out_ref, acc):
+def gather_sum_kernel(ids, got_ref, out_ref, acc, more):
     acc[...] = jnp.zeros_like(acc)
+    more[...] = jnp.zeros_like(more)
 
     def add(q, c):
-        k = ids[lax.div(q, PAIRS), lax.rem(q, PAIRS)]
+        k, n = ids[0, q], ids[1, q]
         for h in (0, 1):
-            acc[k, :, h * 128 : (h + 1) * 128] += got_ref[h, q].astype(F32)
+            acc[h, k] += got_ref[h, q].astype(F32)
+            more[h, n] += got_ref[h, PAIRS + q].astype(F32)
         return c
 
-    lax.fori_loop(0, 2 * PAIRS, add, 0, unroll=8)
-    out_ref[...] = acc[0:BLOCKS].astype(BF16)
+    lax.fori_loop(0, PAIRS, add, 0, unroll=8)
+    for h in (0, 1):
+        out_ref[:, :, h * 128 : (h + 1) * 128] = (acc[h, 0:BLOCKS] + more[h, 0:BLOCKS]).astype(BF16)
 
 
 def gather_sum(ids, arrived):
@@ -100,7 +112,7 @@
         out_shape=jax.ShapeDtypeStruct((BLOCKS, BT, CH), BF16),
         in_specs=[SM, VM],
         out_specs=VM,
-        scratch_shapes=[pltpu.VMEM((BLOCKS + 1, BT, CH), F32)],
+        scratch_shapes=[pltpu.VMEM((2, BLOCKS + 1, BT, 128), F32)] * 2,
         compiler_params=params(),
         cost_estimate=pl.CostEstimate(flops=2**21, bytes_accessed=3 * 2**20, transcendentals=0),
     )(ids, arrived)
@@ -110,7 +122,7 @@
     return lax.axis_index("tile"), lax.axis_index("band"), lax.axis_size("tile"), lax.axis_size("band")
 
 
-def greet(others=0):
+def greet():
     t, b, tiles, bands = place_in_mesh()
     barrier = pltpu.get_barrier_semaphore()
     for dt in (1, -1, 0):
@@ -124,8 +136,12 @@
                 )
 
             near_band(b, bands, db, say)
+
+
+def greet_wait(others):
+    b, bands = lax.axis_index("band"), lax.axis_size("band")
     near = 2 + jnp.where(b > 0, 3, 0) + jnp.where(b < bands - 1, 3, 0)
-    pl.semaphore_wait(barrier, near + others)
+    pl.semaphore_wait(pltpu.get_barrier_semaphore(), near + others)
 
 
 def near_band(b, bands, db, action):
@@ -300,6 +316,58 @@
     lax.fori_loop(0, ROWS + 2 * d, one, 0)
 
 
+def widen_own(ext, wide, first, count):
+    col = lax.broadcasted_iota(jnp.int32, (COLS, CH), 0)
+
+    def one(row, carry):
+        mid = ext[row]
+        x = mid.astype(F32)
+        left = jnp.where(col == 0, 0.0, pltpu.roll(x, 1, 0))
+        right = jnp.where(col == COLS - 1, 0.0, pltpu.roll(x, COLS - 1, 0))
+        at = pl.ds(pl.multiple_of(row * COLS, COLS), COLS)
+        wide[at, 0:CH] = left.astype(BF16)
+        wide[at, CH : 2 * CH] = mid
+        wide[at, 2 * CH : 3 * CH] = right.astype(BF16)
+        return carry
+
+    lax.fori_loop(first, first + count, one, 0)
+
+
+def side_part(rim, turned_rim, taps, out):
+    total = None
+    none = jnp.zeros((ROWS, CH), F32)
+    for i in range(3):
+        near = [rim[side, 0, i : i + ROWS, :] for side in (0, 1)]
+        turned = [none, none] if turned_rim is None else [turned_rim[side, 0, i : i + ROWS, :] for side in (0, 1)]
+        lhs = jnp.concatenate(
+            [
+                jnp.concatenate([near[0], none, turned[0]], axis=1),
+                jnp.concatenate([turned[1], none, near[1]], axis=1),
+            ],
+            axis=0,
+        )
+        part = jnp.dot(lhs.astype(BF16), taps[i], preferred_element_type=F32)
+        total = part if total is None else total + part
+    for r in range(ROWS):
+        at = r * COLS
+        out[at : at + 1, :] += total[r : r + 1]
+        at = r * COLS + COLS - 1
+        out[at : at + 1, :] += total[ROWS + r : ROWS + r + 1]
+
+
+def patch_sides(wide, rim):
+    row = lax.broadcasted_iota(jnp.int32, (16, CH), 0)
+    for r in range(ROWS + 2):
+        at = r * COLS
+        tile = wide[at : at + 16, 0:CH].astype(F32)
+        near = jnp.broadcast_to(rim[0, 0, r : r + 1, :], (16, CH))
+        wide[at : at + 16, 0:CH] = jnp.where(row == 0, near, tile).astype(BF16)
+        at = r * COLS + COLS - 16
+        tile = wide[at : at + 16, 2 * CH : 3 * CH].astype(F32)
+        near = jnp.broadcast_to(rim[1, 0, r : r + 1, :], (16, CH))
+        wide[at : at + 16, 2 * CH : 3 * CH] = jnp.where(row == 15, near, tile).astype(BF16)
+
+
 def conv_block(wide, d, taps, m, rows):
     total = None
     for i in range(3):
@@ -384,7 +452,7 @@
 
 class Swap:
     def __init__(self, bufs, sems):
-        self.bufs, self.sems = bufs, sems
+        self.bufs, self.sems, self.come = bufs, sems, set()
         t, b, tiles, bands = place_in_mesh()
         self.place = spot(t, b)
 
@@ -434,6 +502,14 @@
             self.hop(stage, u, k).wait_recv()
         self.own(stage, u).wait()
 
+    def advance(self, stage, u):
+        if stage > 0:
+            self.wait(stage - 1, u)
+        elif UNITS[u][0] not in self.come:
+            self.come.add(UNITS[u][0])
+            self.core_wait(UNITS[u][0])
+        self.start(stage, u)
+
     def first_stage(self):
         done = set()
         for u in range(8):
@@ -452,10 +528,11 @@
         for u in range(8):
             self.wait(2, u)
 
-    def drain(self):
-        for hs in range(4):
-            self.core_copy(hs).wait_send()
-        for stage in range(3):
+    def drain(self, *stages):
+        for stage in stages:
+            if stage == 0:
+                for hs in range(4):
+                    self.core_copy(hs).wait_send()
             for u in range(8):
                 for k in (1, 2, 3):
                     self.hop(stage, u, k).wait_send()
@@ -517,6 +594,9 @@
 ):
     d = 2
     swap = Swap((outgoing, b1, b2, b3, arrived), sems)
+    greet_table()
+    greet_axes()
+    greet()
     t, b, tiles, bands = place_in_mesh()
     tab[t * 4 + b] = tgt_ref[...] * BLOCKS + blk_ref[...]
     me, before, after = flags(flip)
@@ -524,9 +604,7 @@
     make_slab(ext, d, send, 0, me, tmp)
     clear_edges(ext, d)
     clear_groups(recv)
-    greet_table()
-    greet_axes()
-    greet(sum(TABLE_PEERS) + AXIS_PEERS)
+    greet_wait(sum(TABLE_PEERS) + AXIS_PEERS)
     table_start(tab, tss, trs, 0)
     start_sides(send, recv, ss, rs)
     start_rows(ext, d, rss, rrs)
@@ -585,8 +663,9 @@
     safe_ref[1:2, :] = id_last
     wait_sides_send(send, recv, ss, rs)
     wait_rows_send(ext, d, rss, rrs)
+    swap.drain(0, 1)
     swap.last_wait()
-    swap.drain()
+    swap.drain(2)
 
 
 def back(flip, target, block, source, weights, grad, k1, k2, outgoing):
@@ -631,6 +710,9 @@
     )(flip, target, block, source, weights, grad, k1, k2, outgoing)
 
 
+ORDER = "H a012 K0 a345 K1 20 K2 21 a67 22 b012 30 b345 M b67 31 32 W c012 4012 c345 5012 c67 6012 x d01234567 S 7012 y"
+
+
 def mid_kernel(
     flip, ids, slot, x_ref, hg_ref, g_ref, k1_ref, k1t_ref, k2_ref, w_ref, ps_ref,
     mixed_ref, out_ref, source_ref,
@@ -642,6 +724,8 @@
 ):
     swap = Swap((b0, b1, b2, b3, b4), sems)
     sums = Sums(out_ref, acc, send1, recv1, sent2, got2, sent3, got3, got4, (s1, r1, s2, r2, s3, r3, s4, r4, s5, r5, s6, r6, s7, r7))
+    greet_axes()
+    greet()
     me, before, after = flags(flip)
     ext[pl.ds(1, ROWS)] = x_ref[...]
     make_slab(ext, 1, send, 0, me, tmp)
@@ -650,18 +734,28 @@
     clear_edges(extp, 1)
     clear_groups(recv)
     clear_groups(recv2)
-    greet_axes()
-    greet(AXIS_PEERS)
+    greet_wait(AXIS_PEERS)
     start_sides(send, recv, ss, rs)
     start_rows(ext, 1, rss, rrs)
+    widen_own(ext, wide1_ref, 1, ROWS)
+
+    def inner_pre(n, carry):
+        m = pl.multiple_of(COLS + n * STEP, COLS)
+        ing[pl.ds(m, STEP), :] = conv_block(wide1_ref, 1, k1_ref, m, STEP)
+        return carry
+
+    lax.fori_loop(0, 3, inner_pre, 0)
     wait_sides_recv(send, recv, ss, rs)
     wait_rows_recv(ext, 1, rss, rrs)
     open_slab(recv, 1, 0, me, rim)
-    widen(ext, 1, rim, wide1_ref)
+    for edge in (0, ROWS - 1):
+        widen_own(ext, wide1_ref, 0 if edge == 0 else ROWS + 1, 1)
+        ing[edge * COLS : (edge + 1) * COLS, :] = conv_block(wide1_ref, 1, k1_ref, edge * COLS, COLS)
+    side_part(rim, None, k1_ref, ing)
 
     def act(n, carry):
         m = pl.multiple_of(n * STEP, STEP)
-        pre = conv_block(wide1_ref, 1, k1_ref, m, STEP)
+        pre = ing[pl.ds(m, STEP), :]
         s = jax.nn.sigmoid(pre)
         hid = (pre * s).astype(BF16)
         grad = (hg_ref[pl.ds(m, STEP), :] * s * (1.0 + pre * (1.0 - s))).astype(BF16)
@@ -678,19 +772,25 @@
     start_sides(send2, recv2, ss2, rs2)
     start_rows(extp, 1, rssp, rrsp)
     start_rows(exth, 2, rssh, rrsh)
+    widen_own(extp, widep, 1, ROWS)
+
+    def inner_fold(n, carry):
+        m = pl.multiple_of(COLS + n * STEP, COLS)
+        ing[pl.ds(m, STEP), :] = g_ref[pl.ds(m, STEP), :].astype(F32) + conv_block(widep, 1, k1t_ref, m, STEP)
+        return carry
+
+    lax.fori_loop(0, 3, inner_fold, 0)
+    patch_sides(wide1_ref, rim)
     wait_sides_recv(send2, recv2, ss2, rs2)
     wait_rows_recv(extp, 1, rssp, rrsp)
     open_slab(recv2, 1, 16, me, rim)
     split_rim(rim, 1, me, before, after, trim)
-    widen(extp, 1, rim, widep)
-
-    def fold(n, carry):
-        m = pl.multiple_of(n * STEP, STEP)
-        ing[pl.ds(m, STEP), :] = g_ref[pl.ds(m, STEP), :].astype(F32) + conv_block(widep, 1, k1t_ref, m, STEP)
-        return carry
-
-    lax.fori_loop(0, CELLS // STEP, fold, 0)
-    turned_part(trim, 1, k1t_ref, ing)
+    for edge in (0, ROWS - 1):
+        widen_own(extp, widep, 0 if edge == 0 else ROWS + 1, 1)
+        ing[edge * COLS : (edge + 1) * COLS, :] = g_ref[edge * COLS : (edge + 1) * COLS, :].astype(F32) + conv_block(
+            widep, 1, k1t_ref, edge * COLS, COLS
+        )
+    side_part(rim, trim, k1t_ref, ing)
     for q in range(4):
         part = ing[q * 256 : (q + 1) * 256, :].astype(BF16)
         rounded[q * 16 : (q + 1) * 16] = part.reshape(16, BT, CH)
@@ -708,11 +808,13 @@
         lax.fori_loop(0, PAIRS, pick, 0, unroll=4)
         swap.core_start(half)
         swap.core_start(2 + half)
-    wait_rows_recv(exth, 2, rssh, rrsh)
-    open_slab(recv2, 2, 0, me, rim2)
-    widen(exth, 2, rim2, wide2_ref)
-    swap.first_stage()
-    for o in range(3):
+
+    def hidden_rows():
+        wait_rows_recv(exth, 2, rssh, rrsh)
+        open_slab(recv2, 2, 0, me, rim2)
+        widen(exth, 2, rim2, wide2_ref)
+
+    def kernel_grads(o):
         acc[1, o] = lax.dot_general(
             wide2_ref[o * 2 * COLS : o * 2 * COLS + CELLS, :],
             g_ref[...],
@@ -726,52 +828,63 @@
             preferred_element_type=F32,
         )
         sums.start(o)
-    sums.to_second()
-    swap.next_stage(1)
-
-    def block(n, carry):
-        m = pl.multiple_of(n * STEP, STEP)
-        mixed_ref[pl.ds(m, STEP), :] = (
-            x_ref[pl.ds(m // COLS, STEP // COLS)].reshape(STEP, CH).astype(F32)
-            + conv_block(wide2_ref, 2, k2_ref, m, STEP)
-        ).astype(BF16)
-        return carry
-
-    lax.fori_loop(0, CELLS // STEP, block, 0)
-    w = w_ref[...]
-    ps = ps_ref[0:1, :]
-    for n in range(SB):
-        wexp[n * BL : (n + 1) * BL, :] = w * (ps == n).astype(F32).astype(BF16)
-    sums.to_third()
-    swap.next_stage(2)
-    sums.to_fourth()
-    sums.to_fifth()
-    sums.to_sixth()
-    swap.last_wait()
-
-    def take(p, carry):
-        q = slot[p]
-        half, t = lax.div(q, PAIRS), lax.rem(q, PAIRS)
-        y, zh, x = lax.div(t, 32), lax.rem(lax.div(t, 16), 2), lax.rem(lax.div(t, 4), 4)
-        zl, c = lax.rem(lax.div(t, 2), 2), lax.rem(t, 2)
-        at = pl.ds(pl.multiple_of(p * BT, BT), BT)
-        rows[at, 0:128] = b4[half, y, zh, x, zl, c]
-        rows[at, 128:256] = b4[2 + half, y, zh, x, zl, c]
-        return carry
-
-    lax.fori_loop(0, PAIRS, take, 0, unroll=4)
-    for m in range(4):
-        source_ref[m * 256 : (m + 1) * 256, :] = jnp.dot(
-            wexp[m * 256 : (m + 1) * 256, :], rows[...], preferred_element_type=F32
-        ).astype(BF16)
-    sums.to_seventh()
+
+    def mixed():
+        def block(n, carry):
+            m = pl.multiple_of(n * STEP, STEP)
+            mixed_ref[pl.ds(m, STEP), :] = (
+                x_ref[pl.ds(m // COLS, STEP // COLS)].reshape(STEP, CH).astype(F32)
+                + conv_block(wide2_ref, 2, k2_ref, m, STEP)
+            ).astype(BF16)
+            return carry
+
+        lax.fori_loop(0, CELLS // STEP, block, 0)
+
+    def spread_weights():
+        w = w_ref[...]
+        ps = ps_ref[0:1, :]
+        for n in range(SB):
+            wexp[n * BL : (n + 1) * BL, :] = w * (ps == n).astype(F32).astype(BF16)
+
+    def source():
+        def take(p, carry):
+            q = slot[p]
+            half, t = lax.div(q, PAIRS), lax.rem(q, PAIRS)
+            y, zh, x = lax.div(t, 32), lax.rem(lax.div(t, 16), 2), lax.rem(lax.div(t, 4), 4)
+            zl, c = lax.rem(lax.div(t, 2), 2), lax.rem(t, 2)
+            at = pl.ds(pl.multiple_of(p * BT, BT), BT)
+            rows[at, 0:128] = b4[half, y, zh, x, zl, c]
+            rows[at, 128:256] = b4[2 + half, y, zh, x, zl, c]
+            return carry
+
+        lax.fori_loop(0, PAIRS, take, 0, unroll=4)
+        for m in range(4):
+            source_ref[m * 256 : (m + 1) * 256, :] = jnp.dot(
+                wexp[m * 256 : (m + 1) * 256, :], rows[...], preferred_element_type=F32
+            ).astype(BF16)
+
+    def drained():
+        wait_sides_send(send, recv, ss, rs)
+        wait_rows_send(ext, 1, rss, rrs)
+        wait_sides_send(send2, recv2, ss2, rs2)
+        wait_rows_send(exth, 2, rssh, rrsh)
+        wait_rows_send(extp, 1, rssp, rrsp)
+        swap.drain(0, 1)
+
+    steps = {
+        "x": drained, "y": lambda: swap.drain(2),
+        "H": hidden_rows, "K": kernel_grads, "M": mixed, "W": spread_weights, "S": source,
+        "a": lambda u: swap.advance(0, u), "b": lambda u: swap.advance(1, u),
+        "c": lambda u: swap.advance(2, u), "d": lambda u: swap.wait(2, u),
+        "2": sums.to_second, "3": sums.to_third, "4": sums.to_fourth,
+        "5": sums.to_fifth, "6": sums.to_sixth, "7": sums.to_seventh,
+    }
+    for word in ORDER.split():
+        if len(word) == 1:
+            steps[word]()
+        for n in word[1:]:
+            steps[word[0]](int(n))
     sums.finish()
-    wait_sides_send(send, recv, ss, rs)
-    wait_rows_send(ext, 1, rss, rrs)
-    wait_sides_send(send2, recv2, ss2, rs2)
-    wait_rows_send(exth, 2, rssh, rrsh)
-    wait_rows_send(extp, 1, rssp, rrsp)
-    swap.drain()
 
 
 def mid(flip, ids, slot, x, hidden_grad, grad, k1, k1t, k2, w_cells, ps_cells):
@@ -888,70 +1001,63 @@
         self.send1[o] = self.acc[1 - self.core, o].astype(BF16)
         self.first(o).start()
 
-    def to_second(self):
-        for o in range(3):
-            self.first(o).wait_recv()
-            total = self.acc[self.core, o] + self.recv1[o].astype(F32)
-            self.acc[self.core, o] = total
-            self.sent2[o] = total.astype(BF16)
-            for k in (2, 1, 3):
-                self.second(o, k).start()
-
-    def to_third(self):
-        for o in range(3):
-            for k in (1, 2, 3):
-                self.second(o, k).wait_recv()
-            total = self.acc[self.core, o, self.rows(o, True), :]
-            for k in (1, 2, 3):
-                total = total + self.got2[o, k - 1].astype(F32)
-            self.acc[self.core, o, 0:192, :] = total
-            self.sent3[o] = total.astype(BF16)
-            for k in (2, 1, 3):
-                self.third(o, k).start()
-
-    def to_fourth(self):
-        for o in range(3):
-            a, c, e = axes_of(o)
-            for k in (1, 2, 3):
-                self.third(o, k).wait_recv()
-            total = self.acc[self.core, o, pl.ds(pl.multiple_of(self.place[c] * 48, 16), 48), :]
-            for k in (1, 2, 3):
-                total = total + self.got3[o, k - 1].astype(F32)
-            self.got4[o, self.place[e]] = total.astype(BF16)
-            for k in (2, 1, 3):
-                self.fourth(o, k).start()
-
-    def to_fifth(self):
-        for o in range(3):
-            for k in (1, 2, 3):
-                self.fourth(o, k).wait_recv()
-            v = [self.got4[o, q].astype(F32) for q in range(4)]
-            self.out[self.core, o, self.rows(o, False), :] = (((v[0] + v[1]) + v[2]) + v[3]).astype(BF16)
-            for k in (2, 1, 3):
-                self.fifth(o, k).start()
-
-    def to_sixth(self):
-        for o in range(3):
-            for k in (1, 2, 3):
-                self.fifth(o, k).wait_recv()
-            for k in (2, 1, 3):
-                self.sixth(o, k).start()
-
-    def to_seventh(self):
-        for o in range(3):
-            for k in (1, 2, 3):
-                self.sixth(o, k).wait_recv()
-            self.seventh(o).start()
+    def to_second(self, o):
+        self.first(o).wait_recv()
+        total = self.acc[self.core, o] + self.recv1[o].astype(F32)
+        self.acc[self.core, o] = total
+        self.sent2[o] = total.astype(BF16)
+        for k in (2, 1, 3):
+            self.second(o, k).start()
+
+    def to_third(self, o):
+        for k in (1, 2, 3):
+            self.second(o, k).wait_recv()
+        total = self.acc[self.core, o, self.rows(o, True), :]
+        for k in (1, 2, 3):
+            total = total + self.got2[o, k - 1].astype(F32)
+        self.acc[self.core, o, 0:192, :] = total
+        self.sent3[o] = total.astype(BF16)
+        for k in (2, 1, 3):
+            self.third(o, k).start()
+
+    def to_fourth(self, o):
+        a, c, e = axes_of(o)
+        for k in (1, 2, 3):
+            self.third(o, k).wait_recv()
+        total = self.acc[self.core, o, pl.ds(pl.multiple_of(self.place[c] * 48, 16), 48), :]
+        for k in (1, 2, 3):
+            total = total + self.got3[o, k - 1].astype(F32)
+        self.got4[o, self.place[e]] = total.astype(BF16)
+        for k in (2, 1, 3):
+            self.fourth(o, k).start()
+
+    def to_fifth(self, o):
+        for k in (1, 2, 3):
+            self.fourth(o, k).wait_recv()
+        v = [self.got4[o, q].astype(F32) for q in range(4)]
+        self.out[self.core, o, self.rows(o, False), :] = (((v[0] + v[1]) + v[2]) + v[3]).astype(BF16)
+        for k in (2, 1, 3):
+            self.fifth(o, k).start()
+
+    def to_sixth(self, o):
+        for k in (1, 2, 3):
+            self.fifth(o, k).wait_recv()
+        for k in (2, 1, 3):
+            self.sixth(o, k).start()
+
+    def to_seventh(self, o):
+        for k in (1, 2, 3):
+            self.sixth(o, k).wait_recv()
+        self.seventh(o).start()
 
     def finish(self):
         for o in range(3):
-            self.seventh(o).wait_recv()
-        for o in range(3):
             self.first(o).wait_send()
-            self.seventh(o).wait_send()
             for k in (1, 2, 3):
                 for step in (self.second, self.third, self.fourth, self.fifth, self.sixth):
                     step(o, k).wait_send()
+        for o in range(3):
+            self.seventh(o).wait()
 
 
 def finish_kernel(sums, mixed, source, one, two, mixed_out, source_out, wide, sems):

time: 128 us -> 119 us (0.930)
  Pallas kernels: 123 us -> 114 us
    pallas_call x1, Pallas kernels: 71.4 us -> 66.3 us  [mid(): pl.pallas_call(mid_kernel, name='middle', out_shape=(jax.ShapeDtypeStruct...]
    pallas_call x1, Pallas kernels: 7.26 us -> 3.33 us  [regrid(): pl.pallas_call(regrid_kernel, name='regrid', out_shape=(jax.ShapeDtypeStr...]
where the time goes in v3:
time: 119 us; the launch traced here: 118 us
  Pallas kernels  114 us (96%)
  local copies, waits for them, and re-layouts  3.75 us (3%)
    pallas_call x1, Pallas kernels, mid(): pl.pallas_call(mid_kernel, name='middle', out_shape=(jax.ShapeDtypeStruct...  66.3 us
    pallas_call x1, Pallas kernels, back(): pl.pallas_call(back_kernel, name='hidden_adjoint', out_shape=(jax.ShapeDt...  39.8 us
    unnamed x21, local copies, waits for them, and re-layouts  3.75 us
    pallas_call x1, Pallas kernels, regrid(): pl.pallas_call(regrid_kernel, name='regrid', out_shape=(jax.ShapeDtypeStr...  3.33 us
    pallas_call x1, Pallas kernels, finish(): pl.pallas_call(finish_kernel, name='finish', out_shape=(jax.ShapeDtypeStr...  2.57 us

profile of v3, /device:TPU:1, one launch (start us, length us, event | category | flops | bytes accessed | tf_op | source)
XLA Modules:
  0.0 118.4 jit_solution(16048433299177735772)
XLA Ops:
  0.6 1.4 %copy.14.w_ref = bf16[128,16,64]{2,1,0:T(8,128)(2,1)S(1)} copy(bf16[128,16,64]{0,2,1:T(8,128)(2,1)} %param.10) | data formatting | bytes 524288 | tf_op args[1]
  2.0 0.0 copy-start.2
  2.0 1.0 copy-done.2
  3.1 0.0 copy-start.4
  3.1 0.7 copy-done.4
  3.7 0.0 copy-start.7
  3.7 0.7 copy-done.7
  4.4 0.0 copy-start
  4.4 0.0 copy-start.1
  4.4 0.0 copy-start.3
  4.4 0.0 copy-start.5
  4.4 0.0 copy-start.6
  4.4 0.0 copy-start.8
  4.4 0.0 copy-start.9
  4.4 3.3 %regrid.1 = (bf16[2,256,16,128]{3,2,1,0:T(8,128)(2,1)S(1)}, s32[128]{0:T(128)S(1)}) custom-call(s32[128]{0:T(128)S(1)} %bitcast.20, s32[128]{0:T(128)S(1)} %copy-done.7, bf16[128,16,64]{2,1,0:T(8,128)(2,1)S(1)} %copy.14.w_ref, bf16[1024,256]{1,0:T(8,128)(2,1)S(1)} %copy-done.2), custom_call_target="tpu_custom_call" | custom-call | flops 1073741824 | bytes 6291456 | tf_op jit(solution)/shard_map/regrid/pallas_call | solution.py:69
  7.8 0.0 copy-done
  7.8 0.0 copy-done.1
  7.8 0.0 copy-done.3
  7.8 0.0 copy-done.5
  7.8 0.0 copy-done.6
  7.8 0.0 copy-done.8
  7.8 0.0 copy-done.9
  7.8 39.8 %hidden_adjoint.1 = (f32[1024,256]{1,0:T(8,128)S(1)}, bf16[3,768,256]{2,1,0:T(8,128)(2,1)S(1)}, bf16[4,4,2,4,2,2,16,128]{7,6,5,4,3,2,1,0:T(8,128)(2,1)S(1)}, s32...) custom-call(s32[32]{0:T(128)S(1)} %copy-done.9, ...), custom_call_target="tpu_custom_call" | custom-call | flops 6442450944 | bytes 8388608 | tf_op jit(solution)/shard_map/hidden_adjoint/pallas_call | solution.py:673
  47.6 1.7 %gather_sum.1 = bf16[64,16,256]{2,1,0:T(8,128)(2,1)S(1)} custom-call(s32[2,128]{1,0:T(2,128)S(1)} %get-tuple-element.23.ids, bf16[2,256,16,128]{3,2,1,0:T(8,128)(2,1)S(1)} %bitcast.14), custom_call_target="tpu_custom_call" | custom-call | flops 2097152 | bytes 3145728 | tf_op jit(solution)/shard_map/gather_sum/pallas_call | solution.py:109
  49.3 66.3 %middle.1 = (bf16[1024,256]{1,0:T(8,128)(2,1)S(1)}, bf16[2,3,768,256]{3,2,1,0:T(8,128)(2,1)S(1)}, bf16[1024,256]{1,0:T(8,128)(2,1)S(1)}) custom-call(s32[32]{0:T(128)S(1)} %copy-done.9, s32[2,128]{1,0:T(2,128)S(1)} %get-tuple-element.21.ids, s32[128]{0:T(128)S(1)} %get-tuple-element.22.slot, bf16[8,128,256]{2,1,0:T(8,128)(2,1)S(1)} %bitcast.15, ...), custom_call_target="tpu_custom_call" | custom-call | flops 6442450944 | bytes 12582912 | tf_op jit(solution)/shard_map/middle/pallas_call | solution.py:893
  115.7 2.6 %finish.1 = (f32[3,768,256]{2,1,0:T(8,128)}, f32[3,768,256]{2,1,0:T(8,128)}, bf16[1024,256]{1,0:T(8,128)(2,1)}, bf16[1024,256]{1,0:T(8,128)(2,1)}) custom-call(bf16[2,3,768,256]{3,2,1,0:T(8,128)(2,1)S(1)} %get-tuple-element.29.sums, bf16[1024,256]{1,0:T(8,128)(2,1)S(1)} %get-tuple-element.30.mixed, bf16[1024,256]{1,0:T(8,128)(2,1)S(1)} %get-tuple-element.31.source), custom_call_target="tpu_custom_call" | custom-call | flops 1048576 | bytes 8388608 | tf_op jit(solution)/shard_map/finish/pallas_call | solution.py:1082
Async XLA Ops:
  2.0 1.0 copy-start.2
  3.1 0.7 copy-start.4
  3.7 0.7 copy-start.7
  4.4 3.4 %copy-start = (bf16[3,3,256,256]{3,2,1,0:T(8,128)(2,1)S(1)}, bf16[3,3,256,256]{3,2,1,0:T(8,128)(2,1)}, u32[]{:S(2)}) copy-start(bf16[3,3,256,256]{3,2,1,0:T(8,128)(2,1)} %k1_ref.1) | copy-start | bytes 3538948
  4.4 3.4 %copy-start.1 = (bf16[3,3,256,256]{3,2,1,0:T(8,128)(2,1)S(1)}, bf16[3,3,256,256]{3,2,1,0:T(8,128)(2,1)}, u32[]{:S(2)}) copy-start(bf16[3,3,256,256]{3,2,1,0:T(8,128)(2,1)} %k2_ref.1) | copy-start | bytes 3538948
  4.4 3.4 %copy-start.3 = (bf16[1,8,128,256]{3,2,1,0:T(8,128)(2,1)S(1)}, bf16[1,8,128,256]{3,2,1,0:T(8,128)(2,1)}, u32[]{:S(2)}) copy-start(bf16[1,8,128,256]{3,2,1,0:T(8,128)(2,1)} %param.17) | copy-start | bytes 1572868
  4.4 3.4 %copy-start.5 = (s32[128,1]{0,1:T(1,128)S(1)}, s32[128,1]{0,1:T(1,128)}, u32[]{:S(2)}) copy-start(s32[128,1]{0,1:T(1,128)} %param.11) | copy-start | bytes 1540
  4.4 3.4 %copy-start.6 = (s32[128]{0:T(128)S(1)}, s32[128]{0:T(128)}, u32[]{:S(2)}) copy-start(s32[128]{0:T(128)} %param.12) | copy-start | bytes 1540
  4.4 3.4 %copy-start.8 = (s32[128]{0:T(128)S(1)}, s32[128]{0:T(128)}, u32[]{:S(2)}) copy-start(s32[128]{0:T(128)} %psrc_far.1) | copy-start | bytes 1540
  4.4 3.4 %copy-start.9 = (s32[32]{0:T(128)S(1)}, s32[32]{0:T(128)}, u32[]{:S(2)}) copy-start(s32[32]{0:T(128)} %flip.3) | copy-start | bytes 388

commit v4 on v3

--- a/solution.py
+++ b/solution.py
@@ -409,7 +409,7 @@
 
 
 WORLD = (4, 4, 2, 4, 2, 2, BT, 128)
-UNITS = [(hs, c) for c in (0, 1) for hs in range(4)]
+UNITS = [(hs, other) for other in (0, 1) for hs in range(4)]
 
 
 def axis_peer(axis, k):
@@ -436,7 +436,8 @@
 
 
 def along(ref, unit, axis, v):
-    hs, c = UNITS[unit]
+    hs, other = UNITS[unit]
+    c = lax.rem(lax.axis_index("band") + other, 2)
     if axis == 0:
         return ref.at[hs, :, :, v, :, c]
     if axis == 1:
@@ -452,7 +453,7 @@
 
 class Swap:
     def __init__(self, bufs, sems):
-        self.bufs, self.sems, self.come = bufs, sems, set()
+        self.bufs, self.sems = bufs, sems
         t, b, tiles, bands = place_in_mesh()
         self.place = spot(t, b)
 
@@ -464,33 +465,26 @@
             src.at[hs, :, :, :, :, 1 - me], dst.at[hs, :, :, :, :, me], ss.at[hs], rs.at[hs], twin()
         )
 
-    def core_own(self, hs):
-        me = self.place[3]
-        src, dst = self.bufs[0], self.bufs[1]
-        return pltpu.make_async_copy(src.at[hs, :, :, :, :, me], dst.at[hs, :, :, :, :, me], self.sems[2].at[hs])
-
     def core_start(self, hs):
         self.core_copy(hs).start()
-        self.core_own(hs).start()
-
-    def core_wait(self, hs):
-        self.core_copy(hs).wait_recv()
-        self.core_own(hs).wait()
+
+    def source(self, stage, u):
+        return self.bufs[0] if stage == 0 and UNITS[u][1] == 0 else self.bufs[1 + stage]
 
     def hop(self, stage, u, k):
         axis = (u + stage) % 3
         me = self.place[axis]
-        src, dst = self.bufs[1 + stage], self.bufs[2 + stage]
+        src, dst = self.source(stage, u), self.bufs[2 + stage]
         return remote(
             along(src, u, axis, lax.rem(me + k, 4)), along(dst, u, axis, me),
-            self.sems[3].at[stage, u, k - 1], self.sems[4].at[stage, u, k - 1], axis_peer(axis, k),
+            self.sems[2].at[stage, u, k - 1], self.sems[3].at[stage, u, k - 1], axis_peer(axis, k),
         )
 
     def own(self, stage, u):
         axis = (u + stage) % 3
         me = self.place[axis]
-        src, dst = self.bufs[1 + stage], self.bufs[2 + stage]
-        return pltpu.make_async_copy(along(src, u, axis, me), along(dst, u, axis, me), self.sems[5].at[stage, u])
+        src, dst = self.source(stage, u), self.bufs[2 + stage]
+        return pltpu.make_async_copy(along(src, u, axis, me), along(dst, u, axis, me), self.sems[4].at[stage, u])
 
     def start(self, stage, u):
         for k in (2, 1, 3):
@@ -505,19 +499,13 @@
     def advance(self, stage, u):
         if stage > 0:
             self.wait(stage - 1, u)
-        elif UNITS[u][0] not in self.come:
-            self.come.add(UNITS[u][0])
-            self.core_wait(UNITS[u][0])
+        elif UNITS[u][1] == 1:
+            self.core_copy(UNITS[u][0]).wait_recv()
         self.start(stage, u)
 
-    def first_stage(self):
-        done = set()
-        for u in range(8):
-            hs = UNITS[u][0]
-            if hs not in done:
-                self.core_wait(hs)
-                done.add(hs)
-            self.start(0, u)
+    def first_stage(self, units):
+        for u in units:
+            self.advance(0, u)
 
     def next_stage(self, stage):
         for u in range(8):
@@ -540,7 +528,7 @@
 
 def swap_sems():
     dma = pltpu.SemaphoreType.DMA
-    return [dma((4,)), dma((4,)), dma((4,)), dma((3, 8, 3)), dma((3, 8, 3)), dma((3, 8))]
+    return [dma((4,)), dma((4,)), dma((3, 8, 3)), dma((3, 8, 3)), dma((3, 8))]
 
 
 def table_peer(stage, k):
@@ -610,20 +598,21 @@
     start_rows(ext, d, rss, rrs)
     for hs in range(4):
         swap.core_start(hs)
+    swap.first_stage(range(0, 4))
+    table_wait(tab, tss, trs, 0)
+    table_start(tab, tss, trs, 1)
+    swap.first_stage(range(4, 8))
     for i in range(3):
         for j in range(3):
             k2t[i, j * CH : (j + 1) * CH, :] = k2_ref[2 - i, 2 - j].T
-    table_wait(tab, tss, trs, 0)
-    table_start(tab, tss, trs, 1)
-    swap.first_stage()
     wait_sides_recv(send, recv, ss, rs)
     wait_rows_recv(ext, d, rss, rrs)
     open_slab(recv, d, 0, me, rim)
     split_rim(rim, d, me, before, after, trim)
-    widen(ext, d, rim, wide)
     table_wait(tab, tss, trs, 1)
     table_start(tab, tss, trs, 2)
     swap.next_stage(1)
+    widen(ext, d, rim, wide)
 
     def block(n, carry):
         m = pl.multiple_of(n * STEP, STEP)
@@ -631,10 +620,10 @@
         return carry
 
     lax.fori_loop(0, CELLS // STEP, block, 0)
-    turned_part(trim, d, k2t, hg_ref)
     table_wait(tab, tss, trs, 2)
     table_start(tab, tss, trs, 3)
     swap.next_stage(2)
+    turned_part(trim, d, k2t, hg_ref)
     for i in range(3):
         for j in range(3):
             k1t_ref[i, j * CH : (j + 1) * CH, :] = k1_ref[2 - i, 2 - j].T
@@ -710,7 +699,37 @@
     )(flip, target, block, source, weights, grad, k1, k2, outgoing)
 
 
-ORDER = "H a012 K0 a345 K1 20 K2 21 a67 22 b012 30 b345 M b67 31 32 W c012 4012 c345 5012 c67 6012 x d01234567 S 7012 y"
+ORDER = (
+    "a0123",
+    "H",
+    "K0",
+    "a45",
+    "K1",
+    "20",
+    "K2",
+    "21",
+    "a67",
+    "22",
+    "b012",
+    "30",
+    "b345",
+    "M",
+    "b67",
+    "31",
+    "32",
+    "W",
+    "c012",
+    "4012",
+    "c345",
+    "5012",
+    "c67",
+    "6012",
+    "x",
+    "d01234567",
+    "S",
+    "7012",
+    "y",
+)
 
 
 def mid_kernel(
@@ -879,7 +898,7 @@
         "2": sums.to_second, "3": sums.to_third, "4": sums.to_fourth,
         "5": sums.to_fifth, "6": sums.to_sixth, "7": sums.to_seventh,
     }
-    for word in ORDER.split():
+    for word in ORDER:
         if len(word) == 1:
             steps[word]()
         for n in word[1:]:

time: 119 us -> 117 us (0.983)
    pallas_call x1, Pallas kernels: 39.8 us -> 37.5 us  [back(): pl.pallas_call(back_kernel, name='hidden_adjoint', out_shape=(jax.ShapeDt...]
    pallas_call x1, Pallas kernels: 66.3 us -> 67.5 us  [mid(): pl.pallas_call(mid_kernel, name='middle', out_shape=(jax.ShapeDtypeStruct...]
where the time goes in v4:
time: 117 us
  Pallas kernels  113 us (97%)
  local copies, waits for them, and re-layouts  3.75 us (3%)
    pallas_call x1, Pallas kernels, mid(): pl.pallas_call(mid_kernel, name='middle', out_shape=(jax.ShapeDtypeStruct...  67.5 us
    pallas_call x1, Pallas kernels, back(): pl.pallas_call(back_kernel, name='hidden_adjoint', out_shape=(jax.ShapeDt...  37.5 us
    unnamed x21, local copies, waits for them, and re-layouts  3.75 us
    pallas_call x1, Pallas kernels, regrid(): pl.pallas_call(regrid_kernel, name='regrid', out_shape=(jax.ShapeDtypeStr...  3.33 us
    pallas_call x1, Pallas kernels, finish(): pl.pallas_call(finish_kernel, name='finish', out_shape=(jax.ShapeDtypeStr...  2.57 us

profile of v4, /device:TPU:1, one launch (start us, length us, event | category | flops | bytes accessed | tf_op | source)
XLA Modules:
  0.0 117.3 jit_solution(8140415553624282798)
XLA Ops:
  0.6 1.4 %copy.14.w_ref = bf16[128,16,64]{2,1,0:T(8,128)(2,1)S(1)} copy(bf16[128,16,64]{0,2,1:T(8,128)(2,1)} %param.10) | data formatting | bytes 524288 | tf_op args[1]
  2.0 0.0 copy-start.2
  2.0 1.0 copy-done.2
  3.1 0.0 copy-start.4
  3.1 0.7 copy-done.4
  3.7 0.0 copy-start.7
  3.7 0.7 copy-done.7
  4.4 0.0 copy-start
  4.4 0.0 copy-start.1
  4.4 0.0 copy-start.3
  4.4 0.0 copy-start.5
  4.4 0.0 copy-start.6
  4.4 0.0 copy-start.8
  4.4 0.0 copy-start.9
  4.4 3.3 %regrid.1 = (bf16[2,256,16,128]{3,2,1,0:T(8,128)(2,1)S(1)}, s32[128]{0:T(128)S(1)}) custom-call(s32[128]{0:T(128)S(1)} %bitcast.20, s32[128]{0:T(128)S(1)} %copy-done.7, bf16[128,16,64]{2,1,0:T(8,128)(2,1)S(1)} %copy.14.w_ref, bf16[1024,256]{1,0:T(8,128)(2,1)S(1)} %copy-done.2), custom_call_target="tpu_custom_call" | custom-call | flops 1073741824 | bytes 6291456 | tf_op jit(solution)/shard_map/regrid/pallas_call | solution.py:69
  7.8 0.0 copy-done
  7.8 0.0 copy-done.1
  7.8 0.0 copy-done.3
  7.8 0.0 copy-done.5
  7.8 0.0 copy-done.6
  7.8 0.0 copy-done.8
  7.8 0.0 copy-done.9
  7.8 37.5 %hidden_adjoint.1 = (f32[1024,256]{1,0:T(8,128)S(1)}, bf16[3,768,256]{2,1,0:T(8,128)(2,1)S(1)}, bf16[4,4,2,4,2,2,16,128]{7,6,5,4,3,2,1,0:T(8,128)(2,1)S(1)}, s32...) custom-call(s32[32]{0:T(128)S(1)} %copy-done.9, ...), custom_call_target="tpu_custom_call" | custom-call | flops 6442450944 | bytes 8388608 | tf_op jit(solution)/shard_map/hidden_adjoint/pallas_call | solution.py:662
  45.3 1.7 %gather_sum.1 = bf16[64,16,256]{2,1,0:T(8,128)(2,1)S(1)} custom-call(s32[2,128]{1,0:T(2,128)S(1)} %get-tuple-element.23.ids, bf16[2,256,16,128]{3,2,1,0:T(8,128)(2,1)S(1)} %bitcast.14), custom_call_target="tpu_custom_call" | custom-call | flops 2097152 | bytes 3145728 | tf_op jit(solution)/shard_map/gather_sum/pallas_call | solution.py:109
  47.0 67.5 %middle.1 = (bf16[1024,256]{1,0:T(8,128)(2,1)S(1)}, bf16[2,3,768,256]{3,2,1,0:T(8,128)(2,1)S(1)}, bf16[1024,256]{1,0:T(8,128)(2,1)S(1)}) custom-call(s32[32]{0:T(128)S(1)} %copy-done.9, s32[2,128]{1,0:T(2,128)S(1)} %get-tuple-element.21.ids, s32[128]{0:T(128)S(1)} %get-tuple-element.22.slot, bf16[8,128,256]{2,1,0:T(8,128)(2,1)S(1)} %bitcast.15, ...), custom_call_target="tpu_custom_call" | custom-call | flops 6442450944 | bytes 12582912 | tf_op jit(solution)/shard_map/middle/pallas_call | solution.py:912
  114.5 2.6 %finish.1 = (f32[3,768,256]{2,1,0:T(8,128)}, f32[3,768,256]{2,1,0:T(8,128)}, bf16[1024,256]{1,0:T(8,128)(2,1)}, bf16[1024,256]{1,0:T(8,128)(2,1)}) custom-call(bf16[2,3,768,256]{3,2,1,0:T(8,128)(2,1)S(1)} %get-tuple-element.29.sums, bf16[1024,256]{1,0:T(8,128)(2,1)S(1)} %get-tuple-element.30.mixed, bf16[1024,256]{1,0:T(8,128)(2,1)S(1)} %get-tuple-element.31.source), custom_call_target="tpu_custom_call" | custom-call | flops 1048576 | bytes 8388608 | tf_op jit(solution)/shard_map/finish/pallas_call | solution.py:1101
Async XLA Ops:
  2.0 1.0 copy-start.2
  3.1 0.7 copy-start.4
  3.7 0.7 copy-start.7
  4.4 3.4 %copy-start = (bf16[3,3,256,256]{3,2,1,0:T(8,128)(2,1)S(1)}, bf16[3,3,256,256]{3,2,1,0:T(8,128)(2,1)}, u32[]{:S(2)}) copy-start(bf16[3,3,256,256]{3,2,1,0:T(8,128)(2,1)} %k1_ref.1) | copy-start | bytes 3538948
  4.4 3.4 %copy-start.1 = (bf16[3,3,256,256]{3,2,1,0:T(8,128)(2,1)S(1)}, bf16[3,3,256,256]{3,2,1,0:T(8,128)(2,1)}, u32[]{:S(2)}) copy-start(bf16[3,3,256,256]{3,2,1,0:T(8,128)(2,1)} %k2_ref.1) | copy-start | bytes 3538948
  4.4 3.4 %copy-start.3 = (bf16[1,8,128,256]{3,2,1,0:T(8,128)(2,1)S(1)}, bf16[1,8,128,256]{3,2,1,0:T(8,128)(2,1)}, u32[]{:S(2)}) copy-start(bf16[1,8,128,256]{3,2,1,0:T(8,128)(2,1)} %param.17) | copy-start | bytes 1572868
  4.4 3.4 %copy-start.5 = (s32[128,1]{0,1:T(1,128)S(1)}, s32[128,1]{0,1:T(1,128)}, u32[]{:S(2)}) copy-start(s32[128,1]{0,1:T(1,128)} %param.11) | copy-start | bytes 1540
  4.4 3.4 %copy-start.6 = (s32[128]{0:T(128)S(1)}, s32[128]{0:T(128)}, u32[]{:S(2)}) copy-start(s32[128]{0:T(128)} %param.12) | copy-start | bytes 1540
  4.4 3.4 %copy-start.8 = (s32[128]{0:T(128)S(1)}, s32[128]{0:T(128)}, u32[]{:S(2)}) copy-start(s32[128]{0:T(128)} %psrc_far.1) | copy-start | bytes 1540
  4.4 3.4 %copy-start.9 = (s32[32]{0:T(128)S(1)}, s32[32]{0:T(128)}, u32[]{:S(2)}) copy-start(s32[32]{0:T(128)} %flip.3) | copy-start | bytes 388

commit v5 on v4

--- a/solution.py
+++ b/solution.py
@@ -21,11 +21,10 @@
     return pltpu.CompilerParams(vmem_limit_bytes=LIMIT, **more)
 
 
-def regrid_kernel(tgt_far, psrc_far, w_ref, src_far, out_ref, slot_ref, cnt, masks, wexp, tgt, psrc, src_ref, sems):
+def regrid_kernel(pair_far, w_ref, src_far, out_ref, slot_ref, cnt, masks, wexp, pair, src_ref, sems):
     copies = [
-        pltpu.make_async_copy(tgt_far, tgt, sems.at[0]),
-        pltpu.make_async_copy(psrc_far, psrc, sems.at[1]),
-        pltpu.make_async_copy(src_far, src_ref, sems.at[2]),
+        pltpu.make_async_copy(pair_far, pair, sems.at[0]),
+        pltpu.make_async_copy(src_far, src_ref, sems.at[1]),
     ]
     for copy in copies:
         copy.start()
@@ -40,14 +39,14 @@
 
     lax.fori_loop(0, PAIRS, clear, 0, unroll=8)
     copies[0].wait()
-    copies[1].wait()
 
     def place(p, c):
-        t = tgt[p]
+        named = pair[p]
+        t = lax.shift_right_logical(named, 4)
         r = cnt[t]
         cnt[t] = r + 1
         slot_ref[p] = jnp.minimum(r, 1) * PAIRS + t
-        s = psrc[p]
+        s = lax.bitwise_and(named, SB - 1)
         w = w_ref[p]
         ww = jnp.concatenate([w, w], axis=1) * masks[lax.rem(s, 2)]
         row = pl.multiple_of(p * BT, BT)
@@ -56,7 +55,7 @@
         return c
 
     lax.fori_loop(0, PAIRS, place, 0, unroll=8)
-    copies[2].wait()
+    copies[1].wait()
     for m in range(4):
         part = jnp.dot(wexp[m * 512 : (m + 1) * 512, :], src_ref[...], preferred_element_type=F32).astype(BF16)
         for q in range(32):
@@ -65,7 +64,7 @@
                 out_ref[h, at] = part[q * BT : (q + 1) * BT, h * 128 : (h + 1) * 128]
 
 
-def regrid(tgt, psrc, weights, source):
+def regrid(named, weights, source):
     return pl.pallas_call(
         regrid_kernel,
         name="regrid",
@@ -73,20 +72,19 @@
             jax.ShapeDtypeStruct((2, 2 * PAIRS, BT, 128), BF16),
             jax.ShapeDtypeStruct((PAIRS,), jnp.int32),
         ),
-        in_specs=[FAR, FAR, VM, FAR],
+        in_specs=[FAR, VM, FAR],
         out_specs=(VM, SM),
         scratch_shapes=[
             pltpu.SMEM((PAIRS,), jnp.int32),
             pltpu.VMEM((2, BT, 128), BF16),
             pltpu.VMEM((PAIRS * BT, SB * BL), BF16),
             pltpu.SMEM((PAIRS,), jnp.int32),
-            pltpu.SMEM((PAIRS,), jnp.int32),
             pltpu.VMEM((SB * BL, CH), BF16),
-            pltpu.SemaphoreType.DMA((3,)),
+            pltpu.SemaphoreType.DMA((2,)),
         ],
         compiler_params=params(),
         cost_estimate=pl.CostEstimate(flops=2 * 2048 * 1024 * 256, bytes_accessed=6 * 2**20, transcendentals=0),
-    )(tgt, psrc, weights, source)
+    )(named, weights, source)
 
 
 def gather_sum_kernel(ids, got_ref, out_ref, acc, more):
@@ -1118,8 +1116,7 @@
 def local(
     source_cells, regrid_weights, pair_target, pair_block, pair_source, flip_codes, kernel_one, kernel_two, out_grad
 ):
-    target = pair_target[:, 0]
-    outgoing, slot = regrid(target, pair_source, regrid_weights, source_cells)
+    outgoing, slot = regrid(pair_target[:, 0] * SB + pair_source, regrid_weights, source_cells)
     upstream = out_grad[0]
     hidden_grad, k1_back, arrived, ids, safe_ids, w_cells, ps_cells = back(
         flip_codes,

time: 117 us -> 117 us (level)
  local copies, waits for them, and re-layouts: 3.75 us -> 2.44 us
    unnamed x21 -> x17, local copies, waits for them, and re-layouts: 3.75 us -> 2.44 us
where the time goes in v5:
time: 117 us
  Pallas kernels  113 us (97%)
  local copies, waits for them, and re-layouts  2.44 us (2%)
    pallas_call x1, Pallas kernels, mid(): pl.pallas_call(mid_kernel, name='middle', out_shape=(jax.ShapeDtypeStruct...  67.6 us
    pallas_call x1, Pallas kernels, back(): pl.pallas_call(back_kernel, name='hidden_adjoint', out_shape=(jax.ShapeDt...  37.5 us
    pallas_call x1, Pallas kernels, regrid(): pl.pallas_call(regrid_kernel, name='regrid', out_shape=(jax.ShapeDtypeStr...  3.6 us
    pallas_call x1, Pallas kernels, finish(): pl.pallas_call(finish_kernel, name='finish', out_shape=(jax.ShapeDtypeStr...  2.57 us
    unnamed x17, local copies, waits for them, and re-layouts  2.44 us

profile of v5, /device:TPU:1, one launch (start us, length us, event | category | flops | bytes accessed | tf_op | source)
XLA Modules:
  0.0 116.9 jit_solution(5248855280667281542)
XLA Ops:
  0.6 0.7 bitcast_add_fusion.pair_far
  1.3 1.4 %copy.14.w_ref = bf16[128,16,64]{2,1,0:T(8,128)(2,1)S(1)} copy(bf16[128,16,64]{0,2,1:T(8,128)(2,1)} %param.10) | data formatting | bytes 524288 | tf_op args[1]
  2.7 0.0 copy-start.2
  2.7 1.0 copy-done.2
  3.7 0.0 copy-start
  3.7 0.0 copy-start.1
  3.7 0.0 copy-start.3
  3.7 0.0 copy-start.4
  3.7 0.0 copy-start.5
  3.8 0.0 copy-start.6
  3.8 0.0 copy-start.7
  3.8 3.6 %regrid.1 = (bf16[2,256,16,128]{3,2,1,0:T(8,128)(2,1)S(1)}, s32[128]{0:T(128)S(1)}) custom-call(s32[128]{0:T(128)S(1)} %bitcast_add_fusion.pair_far, bf16[128,16,64]{2,1,0:T(8,128)(2,1)S(1)} %copy.14.w_ref, bf16[1024,256]{1,0:T(8,128)(2,1)S(1)} %copy-done.2), custom_call_target="tpu_custom_call" | custom-call | flops 1073741824 | bytes 6291456 | tf_op jit(solution)/shard_map/regrid/pallas_call | solution.py:68
  7.4 0.0 copy-done
  7.4 0.0 copy-done.1
  7.4 0.0 copy-done.3
  7.4 0.0 copy-done.4
  7.4 0.0 copy-done.5
  7.4 0.0 copy-done.6
  7.4 0.0 copy-done.7
  7.5 37.5 %hidden_adjoint.1 = (f32[1024,256]{1,0:T(8,128)S(1)}, bf16[3,768,256]{2,1,0:T(8,128)(2,1)S(1)}, bf16[4,4,2,4,2,2,16,128]{7,6,5,4,3,2,1,0:T(8,128)(2,1)S(1)}, s32...) custom-call(s32[32]{0:T(128)S(1)} %copy-done.7, ...), custom_call_target="tpu_custom_call" | custom-call | flops 6442450944 | bytes 8388608 | tf_op jit(solution)/shard_map/hidden_adjoint/pallas_call | solution.py:660
  44.9 1.7 %gather_sum.1 = bf16[64,16,256]{2,1,0:T(8,128)(2,1)S(1)} custom-call(s32[2,128]{1,0:T(2,128)S(1)} %get-tuple-element.23.ids, bf16[2,256,16,128]{3,2,1,0:T(8,128)(2,1)S(1)} %bitcast.15), custom_call_target="tpu_custom_call" | custom-call | flops 2097152 | bytes 3145728 | tf_op jit(solution)/shard_map/gather_sum/pallas_call | solution.py:107
  46.6 67.6 %middle.1 = (bf16[1024,256]{1,0:T(8,128)(2,1)S(1)}, bf16[2,3,768,256]{3,2,1,0:T(8,128)(2,1)S(1)}, bf16[1024,256]{1,0:T(8,128)(2,1)S(1)}) custom-call(s32[32]{0:T(128)S(1)} %copy-done.7, s32[2,128]{1,0:T(2,128)S(1)} %get-tuple-element.21.ids, s32[128]{0:T(128)S(1)} %get-tuple-element.22.slot, bf16[8,128,256]{2,1,0:T(8,128)(2,1)S(1)} %bitcast.16, ...), custom_call_target="tpu_custom_call" | custom-call | flops 6442450944 | bytes 12582912 | tf_op jit(solution)/shard_map/middle/pallas_call | solution.py:910
  114.2 2.6 %finish.1 = (f32[3,768,256]{2,1,0:T(8,128)}, f32[3,768,256]{2,1,0:T(8,128)}, bf16[1024,256]{1,0:T(8,128)(2,1)}, bf16[1024,256]{1,0:T(8,128)(2,1)}) custom-call(bf16[2,3,768,256]{3,2,1,0:T(8,128)(2,1)S(1)} %get-tuple-element.29.sums, bf16[1024,256]{1,0:T(8,128)(2,1)S(1)} %get-tuple-element.30.mixed, bf16[1024,256]{1,0:T(8,128)(2,1)S(1)} %get-tuple-element.31.source), custom_call_target="tpu_custom_call" | custom-call | flops 1048576 | bytes 8388608 | tf_op jit(solution)/shard_map/finish/pallas_call | solution.py:1099
Async XLA Ops:
  2.7 1.0 copy-start.2
  3.7 3.7 %copy-start = (bf16[3,3,256,256]{3,2,1,0:T(8,128)(2,1)S(1)}, bf16[3,3,256,256]{3,2,1,0:T(8,128)(2,1)}, u32[]{:S(2)}) copy-start(bf16[3,3,256,256]{3,2,1,0:T(8,128)(2,1)} %k1_ref.1) | copy-start | bytes 3538948
  3.7 3.7 %copy-start.1 = (bf16[3,3,256,256]{3,2,1,0:T(8,128)(2,1)S(1)}, bf16[3,3,256,256]{3,2,1,0:T(8,128)(2,1)}, u32[]{:S(2)}) copy-start(bf16[3,3,256,256]{3,2,1,0:T(8,128)(2,1)} %k2_ref.1) | copy-start | bytes 3538948
  3.7 3.7 %copy-start.3 = (bf16[1,8,128,256]{3,2,1,0:T(8,128)(2,1)S(1)}, bf16[1,8,128,256]{3,2,1,0:T(8,128)(2,1)}, u32[]{:S(2)}) copy-start(bf16[1,8,128,256]{3,2,1,0:T(8,128)(2,1)} %param.17) | copy-start | bytes 1572868
  3.7 3.7 %copy-start.4 = (s32[128,1]{0,1:T(1,128)S(1)}, s32[128,1]{0,1:T(1,128)}, u32[]{:S(2)}) copy-start(s32[128,1]{0,1:T(1,128)} %param.11) | copy-start | bytes 1540
  3.7 3.7 %copy-start.5 = (s32[128]{0:T(128)S(1)}, s32[128]{0:T(128)}, u32[]{:S(2)}) copy-start(s32[128]{0:T(128)} %param.12) | copy-start | bytes 1540
  3.8 3.7 %copy-start.6 = (s32[128]{0:T(128)S(1)}, s32[128]{0:T(128)}, u32[]{:S(2)}) copy-start(s32[128]{0:T(128)} %param.13) | copy-start | bytes 1540
  3.8 3.7 %copy-start.7 = (s32[32]{0:T(128)S(1)}, s32[32]{0:T(128)}, u32[]{:S(2)}) copy-start(s32[32]{0:T(128)} %flip.3) | copy-start | bytes 388

commit v6 on v5

--- a/solution.py
+++ b/solution.py
@@ -822,7 +822,7 @@
             b0[2 + half, y, zh, x, zl, c] = block[:, 128:256]
             return carry
 
-        lax.fori_loop(0, PAIRS, pick, 0, unroll=4)
+        lax.fori_loop(0, PAIRS, pick, 0, unroll=16)
         swap.core_start(half)
         swap.core_start(2 + half)
 
@@ -874,7 +874,7 @@
             rows[at, 128:256] = b4[2 + half, y, zh, x, zl, c]
             return carry
 
-        lax.fori_loop(0, PAIRS, take, 0, unroll=4)
+        lax.fori_loop(0, PAIRS, take, 0, unroll=16)
         for m in range(4):
             source_ref[m * 256 : (m + 1) * 256, :] = jnp.dot(
                 wexp[m * 256 : (m + 1) * 256, :], rows[...], preferred_element_type=F32

time: 117 us -> 117 us (level)
  no operation moved by 1% of the time
where the time goes in v6:
time: 117 us
  Pallas kernels  113 us (97%)
  local copies, waits for them, and re-layouts  2.44 us (2%)
    pallas_call x1, Pallas kernels, mid(): pl.pallas_call(mid_kernel, name='middle', out_shape=(jax.ShapeDtypeStruct...  67.2 us
    pallas_call x1, Pallas kernels, back(): pl.pallas_call(back_kernel, name='hidden_adjoint', out_shape=(jax.ShapeDt...  37.5 us
    pallas_call x1, Pallas kernels, regrid(): pl.pallas_call(regrid_kernel, name='regrid', out_shape=(jax.ShapeDtypeStr...  3.6 us
    pallas_call x1, Pallas kernels, finish(): pl.pallas_call(finish_kernel, name='finish', out_shape=(jax.ShapeDtypeStr...  2.57 us
    unnamed x17, local copies, waits for them, and re-layouts  2.44 us

profile of v6, /device:TPU:1, one launch (start us, length us, event | category | flops | bytes accessed | tf_op | source)
XLA Modules:
  0.0 116.6 jit_solution(11109363201261396164)
XLA Ops:
  0.6 0.7 bitcast_add_fusion.pair_far
  1.3 1.4 %copy.14.w_ref = bf16[128,16,64]{2,1,0:T(8,128)(2,1)S(1)} copy(bf16[128,16,64]{0,2,1:T(8,128)(2,1)} %param.10) | data formatting | bytes 524288 | tf_op args[1]
  2.7 0.0 copy-start.2
  2.7 1.0 copy-done.2
  3.7 0.0 copy-start
  3.7 0.0 copy-start.1
  3.7 0.0 copy-start.3
  3.7 0.0 copy-start.4
  3.7 0.0 copy-start.5
  3.8 0.0 copy-start.6
  3.8 0.0 copy-start.7
  3.8 3.6 %regrid.1 = (bf16[2,256,16,128]{3,2,1,0:T(8,128)(2,1)S(1)}, s32[128]{0:T(128)S(1)}) custom-call(s32[128]{0:T(128)S(1)} %bitcast_add_fusion.pair_far, bf16[128,16,64]{2,1,0:T(8,128)(2,1)S(1)} %copy.14.w_ref, bf16[1024,256]{1,0:T(8,128)(2,1)S(1)} %copy-done.2), custom_call_target="tpu_custom_call" | custom-call | flops 1073741824 | bytes 6291456 | tf_op jit(solution)/shard_map/regrid/pallas_call | solution.py:68
  7.4 0.0 copy-done
  7.4 0.0 copy-done.1
  7.4 0.0 copy-done.3
  7.4 0.0 copy-done.4
  7.4 0.0 copy-done.5
  7.4 0.0 copy-done.6
  7.4 0.0 copy-done.7
  7.5 37.5 %hidden_adjoint.1 = (f32[1024,256]{1,0:T(8,128)S(1)}, bf16[3,768,256]{2,1,0:T(8,128)(2,1)S(1)}, bf16[4,4,2,4,2,2,16,128]{7,6,5,4,3,2,1,0:T(8,128)(2,1)S(1)}, s32...) custom-call(s32[32]{0:T(128)S(1)} %copy-done.7, ...), custom_call_target="tpu_custom_call" | custom-call | flops 6442450944 | bytes 8388608 | tf_op jit(solution)/shard_map/hidden_adjoint/pallas_call | solution.py:660
  44.9 1.7 %gather_sum.1 = bf16[64,16,256]{2,1,0:T(8,128)(2,1)S(1)} custom-call(s32[2,128]{1,0:T(2,128)S(1)} %get-tuple-element.23.ids, bf16[2,256,16,128]{3,2,1,0:T(8,128)(2,1)S(1)} %bitcast.15), custom_call_target="tpu_custom_call" | custom-call | flops 2097152 | bytes 3145728 | tf_op jit(solution)/shard_map/gather_sum/pallas_call | solution.py:107
  46.6 67.2 %middle.1 = (bf16[1024,256]{1,0:T(8,128)(2,1)S(1)}, bf16[2,3,768,256]{3,2,1,0:T(8,128)(2,1)S(1)}, bf16[1024,256]{1,0:T(8,128)(2,1)S(1)}) custom-call(s32[32]{0:T(128)S(1)} %copy-done.7, s32[2,128]{1,0:T(2,128)S(1)} %get-tuple-element.21.ids, s32[128]{0:T(128)S(1)} %get-tuple-element.22.slot, bf16[8,128,256]{2,1,0:T(8,128)(2,1)S(1)} %bitcast.16, ...), custom_call_target="tpu_custom_call" | custom-call | flops 6442450944 | bytes 12582912 | tf_op jit(solution)/shard_map/middle/pallas_call | solution.py:910
  113.9 2.6 %finish.1 = (f32[3,768,256]{2,1,0:T(8,128)}, f32[3,768,256]{2,1,0:T(8,128)}, bf16[1024,256]{1,0:T(8,128)(2,1)}, bf16[1024,256]{1,0:T(8,128)(2,1)}) custom-call(bf16[2,3,768,256]{3,2,1,0:T(8,128)(2,1)S(1)} %get-tuple-element.29.sums, bf16[1024,256]{1,0:T(8,128)(2,1)S(1)} %get-tuple-element.30.mixed, bf16[1024,256]{1,0:T(8,128)(2,1)S(1)} %get-tuple-element.31.source), custom_call_target="tpu_custom_call" | custom-call | flops 1048576 | bytes 8388608 | tf_op jit(solution)/shard_map/finish/pallas_call | solution.py:1099
Async XLA Ops:
  2.7 1.0 copy-start.2
  3.7 3.7 %copy-start = (bf16[3,3,256,256]{3,2,1,0:T(8,128)(2,1)S(1)}, bf16[3,3,256,256]{3,2,1,0:T(8,128)(2,1)}, u32[]{:S(2)}) copy-start(bf16[3,3,256,256]{3,2,1,0:T(8,128)(2,1)} %k1_ref.1) | copy-start | bytes 3538948
  3.7 3.7 %copy-start.1 = (bf16[3,3,256,256]{3,2,1,0:T(8,128)(2,1)S(1)}, bf16[3,3,256,256]{3,2,1,0:T(8,128)(2,1)}, u32[]{:S(2)}) copy-start(bf16[3,3,256,256]{3,2,1,0:T(8,128)(2,1)} %k2_ref.1) | copy-start | bytes 3538948
  3.7 3.7 %copy-start.3 = (bf16[1,8,128,256]{3,2,1,0:T(8,128)(2,1)S(1)}, bf16[1,8,128,256]{3,2,1,0:T(8,128)(2,1)}, u32[]{:S(2)}) copy-start(bf16[1,8,128,256]{3,2,1,0:T(8,128)(2,1)} %param.17) | copy-start | bytes 1572868
  3.7 3.7 %copy-start.4 = (s32[128,1]{0,1:T(1,128)S(1)}, s32[128,1]{0,1:T(1,128)}, u32[]{:S(2)}) copy-start(s32[128,1]{0,1:T(1,128)} %param.11) | copy-start | bytes 1540
  3.7 3.7 %copy-start.5 = (s32[128]{0:T(128)S(1)}, s32[128]{0:T(128)}, u32[]{:S(2)}) copy-start(s32[128]{0:T(128)} %param.12) | copy-start | bytes 1540
  3.8 3.7 %copy-start.6 = (s32[128]{0:T(128)S(1)}, s32[128]{0:T(128)}, u32[]{:S(2)}) copy-start(s32[128]{0:T(128)} %param.13) | copy-start | bytes 1540
  3.8 3.7 %copy-start.7 = (s32[32]{0:T(128)S(1)}, s32[32]{0:T(128)}, u32[]{:S(2)}) copy-start(s32[32]{0:T(128)} %flip.3) | copy-start | bytes 388
